TPU v7x, 32 devices: a whole 2x2x4 slice. The times are simulated.
32 devices in a mesh: parts: 2 (over y), cell: 4 (over z), grp: 4 (over x, core).
Axes of the slice: x: 2, y: 2, z: 4, core: 2. Of those that a mesh axis runs over, the one named last changes fastest.
Arguments:
- sketch: bfloat16 [98304, 256], P(('parts', 'cell', 'grp')), parts along dimension 0, may hold values from -0.27063294 to 0.27063294, as said below
- slab: bfloat16 [98304, 128], P(('parts', 'cell', 'grp')), parts along dimension 0, may hold values from -6 to 6
Outputs:
- r_factor: float32 [512, 256], P('parts'), parts along dimension 0
- basis: bfloat16 [98304, 256], P(('parts', 'cell', 'grp')), parts along dimension 0
- projected: float32 [512, 128], P(('parts', 'cell'), 'grp'), parts along dimension 0
There are 2 independent parts, one for each index of `parts`. A program takes and returns all parts, laid end to end along the dimension named above; each array names one. Nothing has to cross between parts.
Inputs may be any that keep to these rules, and one draw needn't show every extreme that they name: A scaled random sketch of full column rank.
All inputs are finite; a program needn't handle non-finite values.
Results may differ from a plain program's by a relative error of at most 0.001.
Values sent between devices are 32-bit elements; how exact they have to be, the bound alone decides.
No kernel may reach another device: no remote copies, remote signals or barrier semaphores. Data moves between devices by JAX's collectives and lax.ppermute only.
A program may use at most 64 MiB of HBM per device.

v0:
```python
import jax
import jax.numpy as jnp
from jax import lax
from jax.sharding import PartitionSpec as P


def gram_of(piece):
    return lax.dot_general(
        piece, piece, (((0,), (0,)), ((), ())), preferred_element_type=jnp.float32
    )


def local(sketch, slab):
    own_gram = gram_of(sketch)
    own_cross = lax.dot_general(
        sketch, slab, (((0,), (0,)), ((), ())), preferred_element_type=jnp.float32
    )
    total_gram, total_cross = lax.psum((own_gram, own_cross), ("cell", "grp"))
    lower_factor = jnp.linalg.cholesky(total_gram)
    whole_proj = lax.linalg.triangular_solve(lower_factor, total_cross, left_side=True, lower=True)
    row_count = whole_proj.shape[0] // lax.axis_size("cell")
    col_count = whole_proj.shape[1] // lax.axis_size("grp")
    row_start = lax.axis_index("cell") * row_count
    col_start = lax.axis_index("grp") * col_count
    projected = lax.dynamic_slice(whole_proj, (row_start, col_start), (row_count, col_count))
    identity = jnp.eye(lower_factor.shape[0], dtype=jnp.float32)
    inverse_lower = lax.linalg.triangular_solve(lower_factor, identity, left_side=True, lower=True)
    exact_rows = jnp.dot(
        sketch.astype(jnp.float32),
        inverse_lower.T,
        precision=lax.Precision.HIGHEST,
        preferred_element_type=jnp.float32,
    )
    basis = exact_rows.astype(jnp.bfloat16)
    return (lower_factor.T, basis, projected)


def solution(mesh):
    in_specs = (P(("parts", "cell", "grp"), None), P(("parts", "cell", "grp"), None))
    out_specs = (P("parts", None), P(("parts", "cell", "grp"), None), P(("parts", "cell"), "grp"))
    return jax.shard_map(local, mesh=mesh, in_specs=in_specs, out_specs=out_specs, check_vma=False)
```

profile of v0, /device:TPU:0, one launch (start us, length us, event | category | flops | bytes accessed | tf_op | source)
XLA Modules:
  0.0 180.3 jit_solution(13206856936610016307)
XLA Ops:
  7.2 0.0 copy-start
  7.2 0.0 copy-start.1
  7.2 0.0 all-reduce.4.cloned.1.call-start
  7.2 1.3 copy-done
  8.6 1.4 fusion.21
  10.0 0.0 copy-done.1
  10.0 1.3 fusion.22
  11.3 0.0 all-reduce.4.cloned.1.call-update
  11.4 94.1 %all-reduce.4.cloned.1.call-done = (f32[256,256]{0,1:T(8,128)}, f32[256,128]{1,0:T(8,128)}) async-done(((f32[256,256]{0,1:T(8,128)}, f32[256,128]{1,0:T(8,128)}), (f32[256,256]{0,1:T(8,128)}, f32[256,128]{1,0:T(8,128)})) %all-reduce.4.cloned.1.call-update) | async-done | bytes 393232 | tf_op jit(solution)/shard_map/psum | solution.py:18
  105.5 1.1 copy.6
  106.6 1.0 fusion.4
  107.6 11.7 %cholesky.50 = f32[128,128]{1,0:T(8,128)S(1)} custom-call(f32[128,128]{1,0:T(8,128)S(1)} %cholesky.118), custom_call_target="Cholesky" | custom-call | tf_op jit(solution)/shard_map/jit(cholesky)/cholesky | solution.py:19
  119.3 9.8 %custom-call.16 = f32[1,128,128]{1,2,0:T(8,128)S(1)} custom-call(f32[1,128,128]{2,1,0:T(8,128)S(1)} %get-tuple-element.31), custom_call_target="InvertDiagBlocksLowerTriangular" | custom-call | tf_op jit(solution)/shard_map/jit(cholesky)/cholesky | solution.py:19
  129.1 0.0 copy-start.2
  129.2 0.2 constant_dynamic-update-slice_fusion.1
  129.4 0.3 convolution_subtract_fusion.2
  129.7 11.7 %cholesky.105 = f32[128,128]{1,0:T(8,128)S(1)} custom-call(f32[128,128]{1,0:T(8,128)S(1)} %convolution_subtract_fusion.2), custom_call_target="Cholesky" | custom-call | tf_op jit(solution)/shard_map/jit(cholesky)/cholesky | solution.py:19
  141.4 0.6 compare_reduce_fusion
  143.4 0.8 copy.7
  144.2 0.1 triangular_solve.59
  144.3 4.0 %while.1 = (s32[]{:T(128)}, f32[256,256]{1,0:T(8,128)S(1)}, s32[2,2]{1,0:T(2,128)S(1)}, f32[2,128,128]{2,1,0:T(8,128)S(1)}, s32[]{:T(128)}) while((s32[]{:T(128)}, f32[256,256]{1,0:T(8,128)S(1)}, s32[2,2]{1,0:T(2,128)S(1)}, f32[2,128,128]{2,1,0:T(8,128)S(1)}, s32[]{:T(128)}) %tuple.29), condition=%wide.while_cond, body=%wide.while_body.sunk | while | flops 2 | bytes 131189 | solution.py:27
  144.3 0.6 fusion.35
  144.9 1.4 bitcast_dynamic-update-slice_fusion.2
  146.3 0.6 fusion.35
  146.9 1.4 bitcast_dynamic-update-slice_fusion.2
  148.3 19.7 %custom-call.17 = f32[2,128,128]{1,2,0:T(8,128)S(1)} custom-call(f32[2,128,128]{2,1,0:T(8,128)S(1)} %get-tuple-element.10), custom_call_target="InvertDiagBlocksLowerTriangular" | custom-call | tf_op jit(solution)/shard_map/triangular_solve | solution.py:27
  168.0 0.0 copy-done.2
  168.0 0.3 fusion.9
  168.3 0.2 convolution_subtract_fusion.1
  168.5 0.3 fusion.14
  168.8 0.1 fusion.18
  168.9 0.7 copy.9
  169.6 0.3 fusion.7
  169.8 0.3 convolution_subtract_fusion
  170.1 0.3 fusion.15
  170.4 1.4 fusion
  171.9 1.6 copy.8
  (10 shorter events, 0.2 us)
Async XLA Ops:
  7.2 1.4 copy-start
  7.2 2.8 %copy-start.1 = (bf16[3072,128]{1,0:T(8,128)(2,1)S(1)}, bf16[3072,128]{1,0:T(8,128)(2,1)}, u32[]{:S(2)}) copy-start(bf16[3072,128]{1,0:T(8,128)(2,1)} %param.3) | copy-start | bytes 2359300
  7.2 98.3 %all-reduce.4.cloned.1.call-start = ((), (), s32[]{:S(2)}) async-start(), calls=%async_computation | async-start | bytes 786432 | tf_op jit(solution)/shard_map/psum | solution.py:18
  129.1 38.8 %copy-start.2 = (f32[256,128]{1,0:T(8,128)S(1)}, f32[256,128]{1,0:T(8,128)}, u32[]{:S(2)}) copy-start(f32[256,128]{1,0:T(8,128)} %get-tuple-element.23) | copy-start | bytes 393220
Sparse Core Ops, SparseCore 0:
  12.1 93.3 all-reduce.3
where the time goes:
time: 181 us; the launch traced here: 180 us
  waiting for transfers between devices  94.1 us (52%)
  other arithmetic  54.8 us (30%)
  between operations  15.5 us (9%)
  local copies, waits for them, and re-layouts  9.57 us (5%)
  matrix products  6.21 us (3%)
    psum x1, waiting for transfers between devices, local(): total_gram, total_cross = lax.psum((own_gram, own_cross), ('cell', 'grp'))  94.1 us
    another operation x6, other arithmetic, local(): lower_factor = jnp.linalg.cholesky(total_gram)  34 us
    another operation x3, other arithmetic, local(): lax.linalg.triangular_solve(lower_factor, identity, left_side=True, lower...  19.7 us
    unnamed x9, local copies, waits for them, and re-layouts  4.44 us
    another operation x6, local copies, waits for them, and re-layouts  3.95 us
  transfers between devices with their start and end apart: 1, of which 1 were waited for; matrix products, arithmetic and copies ran while one was open for 0% of the time, Pallas kernels for 0%

commit v1 on v0

v1 whole, which is shorter than its diff:
```python
import functools

import jax
import jax.numpy as jnp
from jax import lax
from jax.experimental import pallas as pl
from jax.experimental.pallas import tpu as pltpu
from jax.sharding import PartitionSpec as P

SUB, LANES = 8, 128
HIGHEST = lax.Precision.HIGHEST


def chunks_of(rows, wanted):
    while rows % (16 * wanted):
        wanted -= 1
    return wanted


def stats_kernel(steps, sketch_hbm, slab_hbm, gram_ref, cross_ref, sketch, slab, sems):
    size = sketch.shape[0] // steps
    copies = []
    for step in range(steps):
        rows = pl.ds(step * size, size)
        pair = []
        for which, (src, dst) in enumerate(((sketch_hbm, sketch), (slab_hbm, slab))):
            copy = pltpu.make_async_copy(src.at[rows], dst.at[rows], sems.at[which, step])
            copy.start()
            pair.append(copy)
        copies.append(pair)
    contract = (((0,), (0,)), ((), ()))
    for step in range(steps):
        rows = pl.ds(step * size, size)
        for copy in copies[step]:
            copy.wait()
        part = sketch[rows, :]
        gram = lax.dot_general(part, part, contract, preferred_element_type=jnp.float32)
        cross = lax.dot_general(slab[rows, :], part, contract, preferred_element_type=jnp.float32)
        if step:
            gram, cross = gram_ref[...] + gram, cross_ref[...] + cross
        gram_ref[...] = gram
        cross_ref[...] = cross


def local_stats(sketch, slab):
    rows, k = sketch.shape
    days = slab.shape[1]
    steps = chunks_of(rows, 6)
    hbm = pl.BlockSpec(memory_space=pl.ANY)
    vmem = pl.BlockSpec(memory_space=pltpu.VMEM)
    return pl.pallas_call(
        functools.partial(stats_kernel, steps),
        out_shape=(
            jax.ShapeDtypeStruct((k, k), jnp.float32),
            jax.ShapeDtypeStruct((days, k), jnp.float32),
        ),
        in_specs=[hbm, hbm],
        out_specs=(vmem, vmem),
        scratch_shapes=[
            pltpu.VMEM((rows, k), sketch.dtype),
            pltpu.VMEM((rows, days), slab.dtype),
            pltpu.SemaphoreType.DMA((2, steps)),
        ],
        name="local_stats",
    )(sketch, slab)


def eliminate(a_ref, r_ref, x_ref):
    k = a_ref.shape[0]
    halves = k // LANES
    shape = (SUB, LANES)
    sub = lax.broadcasted_iota(jnp.int32, shape, 0)
    lane = lax.broadcasted_iota(jnp.int32, shape, 1)

    def load(panel):
        rows = pl.ds(panel * SUB, SUB)
        return [a_ref[rows, pl.ds(h * LANES, LANES)] for h in range(halves)]

    def row_of(v, i):
        return jnp.broadcast_to(v[i : i + 1, :], shape)

    def column_of(v, i):
        return jnp.broadcast_to(v[:, i : i + 1], shape)

    for panel in range(k // SUB):
        half, first = divmod(panel * SUB, LANES)
        block = load(panel)
        cols = [column_of(block[half], first + i) for i in range(SUB)]
        saved = [jnp.zeros(shape, jnp.float32)] * halves
        scale = jnp.zeros(shape, jnp.float32)
        for i in range(SUB):
            here = sub == i
            pivot = row_of(cols[i], i)
            inverse = 1.0 / pivot
            root = lax.rsqrt(pivot)
            scale = jnp.where(here, root, scale)
            saved = [jnp.where(here, b, s) for b, s in zip(block, saved)]
            unit = jnp.where(here, 1.0, 0.0)
            block[half] = jnp.where(lane == first + i, unit, block[half])

            def step(v):
                row = row_of(v, i)
                return jnp.where(here, row * inverse, v - (cols[i] * row) * inverse)

            for j in range(i + 1, SUB):
                cols[j] = step(cols[j])
            block = [step(b) for b in block]
        rows = pl.ds(panel * SUB, SUB)
        for h in range(halves):
            at = pl.ds(h * LANES, LANES)
            ahead = lane + h * LANES - (sub + panel * SUB)
            z = saved[h] * scale
            r_ref[rows, at] = jnp.where(ahead >= 0, z, 0.0)
            x_ref[rows, at] = jnp.where(ahead < 0, z, jnp.where(ahead == 0, scale, 0.0))
        pivots = [[row_of(b, i) for b in block] for i in range(SUB)]
        inside = (lane >= first) & (lane < first + SUB)
        for other in range(panel + 1, k // SUB):
            target = load(other)
            coefs = [column_of(target[half], first + i) for i in range(SUB)]
            target[half] = jnp.where(inside, 0.0, target[half])
            rows = pl.ds(other * SUB, SUB)
            for h in range(halves):
                total = coefs[0] * pivots[0][h]
                for i in range(1, SUB):
                    total = total + coefs[i] * pivots[i][h]
                a_ref[rows, pl.ds(h * LANES, LANES)] = target[h] - total


def split3(v):
    high = v.astype(jnp.bfloat16)
    rest = v - high.astype(jnp.float32)
    middle = rest.astype(jnp.bfloat16)
    low = (rest - middle.astype(jnp.float32)).astype(jnp.bfloat16)
    return high, middle, low


def factor_kernel(
    steps, cells, mine_ref, theirs_ref, cross_ref, sketch_hbm, r_ref, basis_hbm, proj_ref,
    a_ref, x_ref, sketch, basis, sem_in, sems,
):
    copy_in = pltpu.make_async_copy(sketch_hbm, sketch, sem_in)
    copy_in.start()
    k = a_ref.shape[0]
    n = k // 2
    core = lax.axis_index("grp") % 2
    first = core == 0
    square = jnp.where(first, mine_ref[0:n, :], theirs_ref[0:n, :])
    packed = jnp.where(first, theirs_ref[0:n, :], mine_ref[0:n, :])
    diagonal = jnp.where(first, theirs_ref[n : n + 1, :], mine_ref[n : n + 1, :])
    turned = packed.T
    row = lax.broadcasted_iota(jnp.int32, (n, n), 0)
    col = lax.broadcasted_iota(jnp.int32, (n, n), 1)
    a_ref[0:n, 0:n] = jnp.where(row >= col, packed, turned)
    a_ref[0:n, n:k] = square.T
    a_ref[n:k, 0:n] = square
    a_ref[n:k, n:k] = jnp.where(
        row < col, packed, jnp.where(row > col, turned, jnp.broadcast_to(diagonal, (n, n)))
    )
    eliminate(a_ref, r_ref, x_ref)
    x = x_ref[...]
    count = k // cells
    start = pl.multiple_of(lax.axis_index("cell") * count, count)
    proj_ref[...] = lax.dot_general(
        x_ref[pl.ds(start, count), :],
        cross_ref[...],
        (((1,), (1,)), ((), ())),
        precision=HIGHEST,
        preferred_element_type=jnp.float32,
    )
    parts = split3(x)
    copy_in.wait()
    size = sketch.shape[0] // steps
    copies = []
    for step in range(steps):
        rows = pl.ds(step * size, size)
        piece = sketch[rows, :]
        total = None
        for part in parts[::-1]:
            term = lax.dot_general(
                piece, part, (((1,), (1,)), ((), ())), preferred_element_type=jnp.float32
            )
            total = term if total is None else total + term
        basis[rows, :] = total.astype(basis.dtype)
        copy = pltpu.make_async_copy(basis.at[rows], basis_hbm.at[rows], sems.at[step])
        copy.start()
        copies.append(copy)
    for copy in copies:
        copy.wait()


def factor(mine, theirs, cross, sketch, cells):
    rows, k = sketch.shape
    steps = chunks_of(rows, 6)
    hbm = pl.BlockSpec(memory_space=pl.ANY)
    vmem = pl.BlockSpec(memory_space=pltpu.VMEM)
    return pl.pallas_call(
        functools.partial(factor_kernel, steps, cells),
        out_shape=(
            jax.ShapeDtypeStruct((k, k), jnp.float32),
            jax.ShapeDtypeStruct((rows, k), jnp.bfloat16),
            jax.ShapeDtypeStruct((k // cells, cross.shape[0]), jnp.float32),
        ),
        in_specs=[vmem, vmem, vmem, hbm],
        out_specs=(vmem, hbm, vmem),
        scratch_shapes=[
            pltpu.VMEM((k, k), jnp.float32),
            pltpu.VMEM((k, k), jnp.float32),
            pltpu.VMEM((rows, k), sketch.dtype),
            pltpu.VMEM((rows, k), jnp.bfloat16),
            pltpu.SemaphoreType.DMA,
            pltpu.SemaphoreType.DMA((steps,)),
        ],
        name="factor",
    )(mine, theirs, cross, sketch)


def swap(value, axis, bit):
    size = lax.axis_size(axis)
    return lax.ppermute(value, axis, [(i, i ^ bit) for i in range(size)])


def halve(days, place, bit):
    groups, rows, k = days.shape
    pairs = days.reshape(groups // 2, 2, rows, k)
    own = (place // bit) % 2
    return (
        lax.dynamic_index_in_dim(pairs, own, 1, keepdims=False),
        lax.dynamic_index_in_dim(pairs, 1 - own, 1, keepdims=False),
    )


def flat(gram, days):
    groups, rows, k = days.shape
    days = days.reshape(groups * rows, k)
    return jnp.concatenate([gram] + [days[:, i : i + LANES] for i in range(0, k, LANES)], 0)


def unflat(both, gram_rows, groups, rows, k):
    count = groups * rows
    days = [both[gram_rows + i * count : gram_rows + (i + 1) * count] for i in range(k // LANES)]
    return both[:gram_rows], jnp.concatenate(days, 1).reshape(groups, rows, k)


def local(sketch, slab):
    cells, groups = lax.axis_size("cell"), lax.axis_size("grp")
    place = lax.axis_index("grp")
    gram, days = local_stats(sketch, slab)
    k = gram.shape[0]
    n = k // 2
    top, low, square = gram[:n, :n], gram[n:, n:], gram[n:, :n]
    row = lax.broadcasted_iota(jnp.int32, (n, n), 0)
    col = lax.broadcasted_iota(jnp.int32, (n, n), 1)
    packed = jnp.where(row >= col, top, low)
    diagonal = jnp.sum(jnp.where(row == col, low, 0.0), axis=0, keepdims=True)
    extra = jnp.broadcast_to(diagonal, (SUB, n))
    halves = jnp.stack([jnp.concatenate([square, extra], 0), jnp.concatenate([packed, extra], 0)])
    core = place % 2
    kept = lax.dynamic_index_in_dim(halves, core, 0, keepdims=False)
    sent = lax.dynamic_index_in_dim(halves, 1 - core, 0, keepdims=False)
    days = days.reshape(groups, days.shape[0] // groups, k)
    bit = 1
    while bit < groups:
        days_kept, days_sent = halve(days, place, bit)
        if bit == 1:
            gram_kept, gram_sent = kept, sent
        else:
            gram_kept = gram_sent = kept
        got = swap(flat(gram_sent, days_sent), "grp", bit)
        both = flat(gram_kept, days_kept) + got
        kept, days = unflat(both, gram_kept.shape[0], *days_kept.shape)
        bit *= 2
    bit = 1
    while bit < cells:
        both = both + swap(both, "cell", bit)
        bit *= 2
    kept, days = unflat(both, kept.shape[0], *days.shape)
    theirs = swap(kept, "grp", 1)
    r_factor, basis, projected = factor(kept, theirs, days[0], sketch, cells)
    return r_factor, basis, projected


def solution(mesh):
    in_specs = (P(("parts", "cell", "grp"), None), P(("parts", "cell", "grp"), None))
    out_specs = (P("parts", None), P(("parts", "cell", "grp"), None), P(("parts", "cell"), "grp"))
    return jax.shard_map(local, mesh=mesh, in_specs=in_specs, out_specs=out_specs, check_vma=False)
```

time: 181 us -> 43.5 us (0.24)
  waiting for transfers between devices: 94.1 us -> 10.4 us
  other arithmetic: 54.8 us -> 1.69 us
  Pallas kernels: 0 us -> 18.8 us
  between operations: 15.5 us -> 0.8 us
  starting transfers between devices: 0.04 us -> 8.3 us
  local copies, waits for them, and re-layouts: 9.57 us -> 3.02 us
  matrix products: 6.21 us -> 0 us
    psum x1 -> x0, waiting for transfers between devices: 94.1 us -> none  [local(): total_gram, total_cross = lax.psum((own_gram, own_cross), ('cell', 'grp'))]
    another operation x10 -> x1, other arithmetic: 53.8 us -> 0.01 us  [local(): jnp.stack([jnp.concatenate([square, extra], 0), jnp.concatenate([packed,...]
    pallas_call x0 -> x2, Pallas kernels: none -> 18.8 us  [the longest x1 15.6 us: factor(): pl.pallas_call(functools.partial(factor_kernel, steps, cells), out_shape=...]
    ppermute x0 -> x5, waiting for transfers between devices: none -> 10.4 us  [swap(): return lax.ppermute(value, axis, [(i, i ^ bit) for i in range(size)])]
    ppermute x0 -> x5, starting transfers between devices: none -> 8.3 us  [swap(): return lax.ppermute(value, axis, [(i, i ^ bit) for i in range(size)])]
    dot_general x3 -> x0, matrix products: 4.13 us -> none  [the longest x1 1.43 us: local(): jnp.dot(sketch.astype(jnp.float32), inverse_lower.T, precision=lax.Precis...]
    another operation x9 -> x0, local copies, waits for them, and re-layouts: 4.05 us -> none
    unnamed x9 -> x4, local copies, waits for them, and re-layouts: 4.44 us -> 0.63 us
  transfers between devices with their start and end apart: 1 -> 5, of which waited for: 1 -> 5; matrix products, arithmetic and copies ran while one was open for 0% -> 1% of each run, Pallas kernels for 0% -> 0%
where the time goes in v1:
time: 43.5 us; the launch traced here: 43 us
  Pallas kernels  18.8 us (43%)
  waiting for transfers between devices  10.4 us (24%)
  starting transfers between devices  8.3 us (19%)
  local copies, waits for them, and re-layouts  3.02 us (7%)
  other arithmetic  1.69 us (4%)
  between operations  0.8 us (2%)
    pallas_call x1, Pallas kernels, factor(): pl.pallas_call(functools.partial(factor_kernel, steps, cells), out_shape=...  15.6 us
    ppermute x5, waiting for transfers between devices, swap(): return lax.ppermute(value, axis, [(i, i ^ bit) for i in range(size)])  10.4 us
    ppermute x5, starting transfers between devices, swap(): return lax.ppermute(value, axis, [(i, i ^ bit) for i in range(size)])  8.3 us
    pallas_call x1, Pallas kernels, local_stats(): pl.pallas_call(functools.partial(stats_kernel, steps), out_shape=(jax.Sha...  3.22 us
    pallas_call x1, local copies, waits for them, and re-layouts, factor(): pl.pallas_call(functools.partial(factor_kernel, steps, cells), out_shape=...  1.44 us
    select_n x1, other arithmetic, local(): packed = jnp.where(row >= col, top, low)  0.94 us
    dynamic_slice x1, local copies, waits for them, and re-layouts, halve(): lax.dynamic_index_in_dim(pairs, own, 1, keepdims=False)  0.89 us
  transfers between devices with their start and end apart: 5, of which 5 were waited for; matrix products, arithmetic and copies ran while one was open for 1% of the time, Pallas kernels for 0%

profile of v1, /device:TPU:0, one launch (start us, length us, event | category | flops | bytes accessed | tf_op | source)
XLA Modules:
  0.0 43.0 jit_solution(7538278553680277732)
XLA Ops:
  0.6 3.2 %local_stats.1 = (f32[256,256]{1,0:T(8,128)}, f32[128,256]{1,0:T(8,128)}) custom-call(bf16[3072,256]{1,0:T(8,128)(2,1)} %sketch_hbm.3, bf16[3072,128]{1,0:T(8,128)(2,1)} %slab_hbm.1), custom_call_target="tpu_custom_call" | custom-call | tf_op jit(solution)/shard_map/local_stats/pallas_call | solution.py:51
  3.9 0.9 %slice_select_fusion = (f32[128,128]{1,0:T(8,128)S(1)}, f32[128]{0:T(128)S(1)}, f32[128,128]{1,0:T(8,128)S(1)}) fusion(f32[256,256]{1,0:T(8,128)} %get-tuple-element.5), kind=kLoop, calls=%fused_computation.20 | loop fusion | flops 81792 | bytes 328192 | tf_op jit(solution)/shard_map/jit(_where)/select_n | solution.py:253
  4.8 0.9 %constant_dynamic-slice_fusion.1 = (f32[2,1,32,256]{3,2,1,0:T(8,128)S(1)}, f32[2,1,32,256]{3,2,1,0:T(8,128)S(1)}) fusion(f32[2,2,32,256]{3,2,1,0:T(8,128)} %bitcast.23, s32[]{:T(128)S(6)} %select_n.46, s32[]{:T(128)S(6)} %select_n.47), kind=kLoop, calls=%fused_computation.28 | loop fusion | bytes 262152 | tf_op jit(solution)/shard_map/jit(dynamic_index_in_dim)/dynamic_slice | solution.py:227
  5.8 0.5 %collective-permute-start = (f32[264,128]{1,0:T(8,128)S(1)}, f32[264,128]{1,0:T(8,128)S(1)}, u32[]{:S(2)}, u32[]{:S(2)}) collective-permute-start(f32[264,128]{1,0:T(8,128)S(1)} %pad_maximum_fusion), channel_id=1, source_target_pairs={{0,1},{1,0},{2,3},{3,2},{4,5},{5,4},{6,7},{7,6},{8,9},{9,8},{10,11... | collective-permute-start | bytes 405512 | tf_op jit(solution)/shard_map/ppermute | solution.py:219
  6.4 1.0 %collective-permute-done = f32[264,128]{1,0:T(8,128)S(1)} collective-permute-done((f32[264,128]{1,0:T(8,128)S(1)}, f32[264,128]{1,0:T(8,128)S(1)}, u32[]{:S(2)}, u32[]{:S(2)}) %collective-permute-start) | collective-permute-done | bytes 135200 | tf_op jit(solution)/shard_map/ppermute | solution.py:219
  7.5 2.9 %collective-permute-start.1 = (f32[200,128]{1,0:T(8,128)S(1)}, f32[200,128]{1,0:T(8,128)S(1)}, u32[]{:S(2)}, u32[]{:S(2)}) collective-permute-start(f32[200,128]{1,0:T(8,128)S(1)} %fusion.2), channel_id=1, source_target_pairs={{0,2},{1,3},{2,0},{3,1},{4,6},{5,7},{6,4},{7,5},{8,10},{9,11},{10,... | collective-permute-start | bytes 307208 | tf_op jit(solution)/shard_map/ppermute | solution.py:219
  10.4 3.2 %collective-permute-done.1 = f32[200,128]{1,0:T(8,128)S(1)} collective-permute-done((f32[200,128]{1,0:T(8,128)S(1)}, f32[200,128]{1,0:T(8,128)S(1)}, u32[]{:S(2)}, u32[]{:S(2)}) %collective-permute-start.1) | collective-permute-done | bytes 102432 | tf_op jit(solution)/shard_map/ppermute | solution.py:219
  13.6 1.9 %collective-permute-start.2 = (f32[200,128]{1,0:T(8,128)S(1)}, f32[200,128]{1,0:T(8,128)S(1)}, u32[]{:S(2)}, u32[]{:S(2)}) collective-permute-start(f32[200,128]{1,0:T(8,128)S(1)} %fusion.1), channel_id=1, source_target_pairs={{0,4},{4,0},{8,12},{12,8},{1,5},{5,1},{9,13},{13,9},{2,6},{6,2},{1... | collective-permute-start | bytes 307208 | tf_op jit(solution)/shard_map/ppermute | solution.py:219
  15.5 2.8 %collective-permute-done.2 = f32[200,128]{1,0:T(8,128)S(1)} collective-permute-done((f32[200,128]{1,0:T(8,128)S(1)}, f32[200,128]{1,0:T(8,128)S(1)}, u32[]{:S(2)}, u32[]{:S(2)}) %collective-permute-start.2) | collective-permute-done | bytes 102432 | tf_op jit(solution)/shard_map/ppermute | solution.py:219
  18.3 2.9 %collective-permute-start.3 = (f32[200,128]{1,0:T(8,128)S(1)}, f32[200,128]{1,0:T(8,128)S(1)}, u32[]{:S(2)}, u32[]{:S(2)}) collective-permute-start(f32[200,128]{1,0:T(8,128)S(1)} %add.50), channel_id=1, source_target_pairs={{0,8},{4,12},{8,0},{12,4},{1,9},{5,13},{9,1},{13,5},{2,10},{6,14},... | collective-permute-start | bytes 307208 | tf_op jit(solution)/shard_map/ppermute | solution.py:219
  21.2 2.7 %collective-permute-done.3 = f32[200,128]{1,0:T(8,128)S(1)} collective-permute-done((f32[200,128]{1,0:T(8,128)S(1)}, f32[200,128]{1,0:T(8,128)S(1)}, u32[]{:S(2)}, u32[]{:S(2)}) %collective-permute-start.3) | collective-permute-done | bytes 102432 | tf_op jit(solution)/shard_map/ppermute | solution.py:219
  24.0 0.0 copy-start
  24.0 0.1 collective-permute-start.4
  24.1 0.6 %pad_maximum_fusion.6.cross_ref = f32[32,256]{1,0:T(8,128)} fusion(f32[32,128]{1,0:T(8,128)S(1)} %get-tuple-element.20, f32[32,128]{1,0:T(8,128)S(1)} %get-tuple-element.19), kind=kLoop, calls=%fused_computation.24 | loop fusion | flops 8192 | bytes 65536 | tf_op jit(solution)/shard_map/concatenate | solution.py:241
  24.7 0.6 %collective-permute-done.4.theirs_ref = f32[136,128]{1,0:T(8,128)S(1)} collective-permute-done((f32[136,128]{1,0:T(8,128)S(1)}, f32[136,128]{1,0:T(8,128)S(1)}, u32[]{:S(2)}, u32[]{:S(2)}) %collective-permute-start.4) | collective-permute-done | bytes 69664 | tf_op jit(solution)/shard_map/ppermute | solution.py:219
  25.3 0.0 copy-done
  25.3 0.0 copy-start.1
  25.3 0.6 %copy-done.1 = f32[136,128]{1,0:T(8,128)} copy-done((f32[136,128]{1,0:T(8,128)}, f32[136,128]{1,0:T(8,128)S(1)}, u32[]{:S(2)}) %copy-start.1) | copy-done | bytes 69656
  26.0 15.6 %factor.1 = (f32[256,256]{1,0:T(8,128)}, bf16[3072,256]{1,0:T(8,128)(2,1)}, f32[64,32]{1,0:T(8,128)}) custom-call(f32[136,128]{1,0:T(8,128)} %copy-done, f32[136,128]{1,0:T(8,128)} %copy-done.1, f32[32,256]{1,0:T(8,128)} %pad_maximum_fusion.6.cross_ref, bf16[3072,256]{1,0:T(8,128)(2,1)} %sketch_hbm.3), custom_call_target="tpu_custom_call" | custom-call | tf_op jit(solution)/shard_map/factor/pallas_call | solution.py:196
  41.6 1.4 %copy.7 = f32[64,32]{0,1:T(8,128)} copy(f32[64,32]{1,0:T(8,128)} %get-tuple-element.9) | data formatting | bytes 16384 | tf_op jit(solution)/shard_map/factor/pallas_call | solution.py:196
  (19 shorter events, 0.2 us)
Async XLA Ops:
  5.8 1.5 %collective-permute-start = (f32[264,128]{1,0:T(8,128)S(1)}, f32[264,128]{1,0:T(8,128)S(1)}, u32[]{:S(2)}, u32[]{:S(2)}) collective-permute-start(f32[264,128]{1,0:T(8,128)S(1)} %pad_maximum_fusion), channel_id=1, source_target_pairs={{0,1},{1,0},{2,3},{3,2},{4,5},{5,4},{6,7},{7,6},{8,9},{9,8},{10,11... | collective-permute-start | bytes 405512 | tf_op jit(solution)/shard_map/ppermute | solution.py:219
  7.5 6.1 %collective-permute-start.1 = (f32[200,128]{1,0:T(8,128)S(1)}, f32[200,128]{1,0:T(8,128)S(1)}, u32[]{:S(2)}, u32[]{:S(2)}) collective-permute-start(f32[200,128]{1,0:T(8,128)S(1)} %fusion.2), channel_id=1, source_target_pairs={{0,2},{1,3},{2,0},{3,1},{4,6},{5,7},{6,4},{7,5},{8,10},{9,11},{10,... | collective-permute-start | bytes 307208 | tf_op jit(solution)/shard_map/ppermute | solution.py:219
  13.6 4.7 %collective-permute-start.2 = (f32[200,128]{1,0:T(8,128)S(1)}, f32[200,128]{1,0:T(8,128)S(1)}, u32[]{:S(2)}, u32[]{:S(2)}) collective-permute-start(f32[200,128]{1,0:T(8,128)S(1)} %fusion.1), channel_id=1, source_target_pairs={{0,4},{4,0},{8,12},{12,8},{1,5},{5,1},{9,13},{13,9},{2,6},{6,2},{1... | collective-permute-start | bytes 307208 | tf_op jit(solution)/shard_map/ppermute | solution.py:219
  18.3 5.6 %collective-permute-start.3 = (f32[200,128]{1,0:T(8,128)S(1)}, f32[200,128]{1,0:T(8,128)S(1)}, u32[]{:S(2)}, u32[]{:S(2)}) collective-permute-start(f32[200,128]{1,0:T(8,128)S(1)} %add.50), channel_id=1, source_target_pairs={{0,8},{4,12},{8,0},{12,4},{1,9},{5,13},{9,1},{13,5},{2,10},{6,14},... | collective-permute-start | bytes 307208 | tf_op jit(solution)/shard_map/ppermute | solution.py:219
  24.0 1.3 %copy-start = (f32[136,128]{1,0:T(8,128)}, f32[136,128]{1,0:T(8,128)S(1)}, u32[]{:S(2)}) copy-start(f32[136,128]{1,0:T(8,128)S(1)} %slice.79.mine_ref) | copy-start | bytes 208900
  24.0 1.3 %collective-permute-start.4 = (f32[136,128]{1,0:T(8,128)S(1)}, f32[136,128]{1,0:T(8,128)S(1)}, u32[]{:S(2)}, u32[]{:S(2)}) collective-permute-start(f32[136,128]{1,0:T(8,128)S(1)} %slice.79.mine_ref), channel_id=1, source_target_pairs={{0,1},{1,0},{2,3},{3,2},{4,5},{5,4},{6,7},{7,6},{8,9},{9,8},{10,11... | collective-permute-start | bytes 208904 | tf_op jit(solution)/shard_map/ppermute | solution.py:219
  25.3 0.6 %copy-start.1 = (f32[136,128]{1,0:T(8,128)}, f32[136,128]{1,0:T(8,128)S(1)}, u32[]{:S(2)}) copy-start(f32[136,128]{1,0:T(8,128)S(1)} %collective-permute-done.4.theirs_ref) | copy-start | bytes 208900

commit v2 on v1

--- a/solution.py
+++ b/solution.py
@@ -8,6 +8,7 @@
 from jax.sharding import PartitionSpec as P
 
 SUB, LANES = 8, 128
+VMEM_LIMIT = 24 * 2**20
 HIGHEST = lax.Precision.HIGHEST
 
 
@@ -17,7 +18,9 @@
     return wanted
 
 
-def stats_kernel(steps, sketch_hbm, slab_hbm, gram_ref, cross_ref, sketch, slab, sems):
+def stats_kernel(
+    steps, groups, sketch_hbm, slab_hbm, kept_ref, sent_ref, sketch, slab, gram_ref, cross_ref, sems
+):
     size = sketch.shape[0] // steps
     copies = []
     for step in range(steps):
@@ -40,27 +43,50 @@
             gram, cross = gram_ref[...] + gram, cross_ref[...] + cross
         gram_ref[...] = gram
         cross_ref[...] = cross
-
-
-def local_stats(sketch, slab):
+    k = gram_ref.shape[0]
+    n = k // 2
+    first = lax.axis_index("grp") % 2 == 0
+    row = lax.broadcasted_iota(jnp.int32, (n, n), 0)
+    col = lax.broadcasted_iota(jnp.int32, (n, n), 1)
+    square, top, low = gram_ref[n:k, 0:n], gram_ref[0:n, 0:n], gram_ref[n:k, n:k]
+    packed = jnp.where(row >= col, top, low)
+    diagonal = jnp.sum(jnp.where(row == col, low, 0.0), axis=0, keepdims=True)
+    kept_ref[0:n, :] = jnp.where(first, square, packed)
+    sent_ref[0:n, :] = jnp.where(first, packed, square)
+    for ref in (kept_ref, sent_ref):
+        ref[n : n + SUB, :] = jnp.broadcast_to(diagonal, (SUB, n))
+    count = cross_ref.shape[0] // groups
+    at = n + SUB
+    for pair in range(groups // 2):
+        even = pl.ds(2 * pair * count, count)
+        odd = pl.ds((2 * pair + 1) * count, count)
+        for lanes in (pl.ds(h, LANES) for h in range(0, k, LANES)):
+            rows = pl.ds(at, count)
+            kept_ref[rows, :] = jnp.where(first, cross_ref[even, lanes], cross_ref[odd, lanes])
+            sent_ref[rows, :] = jnp.where(first, cross_ref[odd, lanes], cross_ref[even, lanes])
+            at += count
+
+
+def local_stats(sketch, slab, groups):
     rows, k = sketch.shape
     days = slab.shape[1]
     steps = chunks_of(rows, 6)
-    hbm = pl.BlockSpec(memory_space=pl.ANY)
+    hbm = pl.BlockSpec(memory_space=pltpu.HBM)
     vmem = pl.BlockSpec(memory_space=pltpu.VMEM)
+    out = jax.ShapeDtypeStruct((k // 2 + SUB + days // 2 * (k // LANES), LANES), jnp.float32)
     return pl.pallas_call(
-        functools.partial(stats_kernel, steps),
-        out_shape=(
-            jax.ShapeDtypeStruct((k, k), jnp.float32),
-            jax.ShapeDtypeStruct((days, k), jnp.float32),
-        ),
+        functools.partial(stats_kernel, steps, groups),
+        out_shape=(out, out),
         in_specs=[hbm, hbm],
         out_specs=(vmem, vmem),
         scratch_shapes=[
             pltpu.VMEM((rows, k), sketch.dtype),
             pltpu.VMEM((rows, days), slab.dtype),
+            pltpu.VMEM((k, k), jnp.float32),
+            pltpu.VMEM((days, k), jnp.float32),
             pltpu.SemaphoreType.DMA((2, steps)),
         ],
+        compiler_params=pltpu.CompilerParams(vmem_limit_bytes=VMEM_LIMIT),
         name="local_stats",
     )(sketch, slab)
 
@@ -135,7 +161,7 @@
 
 
 def factor_kernel(
-    steps, cells, mine_ref, theirs_ref, cross_ref, sketch_hbm, r_ref, basis_hbm, proj_ref,
+    steps, cells, mine_ref, theirs_ref, sketch_hbm, r_ref, basis_hbm, proj_ref,
     a_ref, x_ref, sketch, basis, sem_in, sems,
 ):
     copy_in = pltpu.make_async_copy(sketch_hbm, sketch, sem_in)
@@ -157,17 +183,23 @@
         row < col, packed, jnp.where(row > col, turned, jnp.broadcast_to(diagonal, (n, n)))
     )
     eliminate(a_ref, r_ref, x_ref)
-    x = x_ref[...]
     count = k // cells
     start = pl.multiple_of(lax.axis_index("cell") * count, count)
-    proj_ref[...] = lax.dot_general(
-        x_ref[pl.ds(start, count), :],
-        cross_ref[...],
-        (((1,), (1,)), ((), ())),
-        precision=HIGHEST,
-        preferred_element_type=jnp.float32,
-    )
-    parts = split3(x)
+    own_rows = pl.ds(start, count)
+    days = proj_ref.shape[0]
+    total = None
+    for h in range(k // LANES):
+        at = n + SUB + h * days
+        term = lax.dot_general(
+            mine_ref[at : at + days, :],
+            x_ref[own_rows, h * LANES : (h + 1) * LANES],
+            (((1,), (1,)), ((), ())),
+            precision=HIGHEST,
+            preferred_element_type=jnp.float32,
+        )
+        total = term if total is None else total + term
+    proj_ref[...] = total
+    parts = split3(x_ref[...])
     copy_in.wait()
     size = sketch.shape[0] // steps
     copies = []
@@ -188,19 +220,20 @@
         copy.wait()
 
 
-def factor(mine, theirs, cross, sketch, cells):
+def factor(mine, theirs, sketch, cells):
     rows, k = sketch.shape
+    days = (mine.shape[0] - theirs.shape[0]) * LANES // k
     steps = chunks_of(rows, 6)
-    hbm = pl.BlockSpec(memory_space=pl.ANY)
+    hbm = pl.BlockSpec(memory_space=pltpu.HBM)
     vmem = pl.BlockSpec(memory_space=pltpu.VMEM)
     return pl.pallas_call(
         functools.partial(factor_kernel, steps, cells),
         out_shape=(
             jax.ShapeDtypeStruct((k, k), jnp.float32),
             jax.ShapeDtypeStruct((rows, k), jnp.bfloat16),
-            jax.ShapeDtypeStruct((k // cells, cross.shape[0]), jnp.float32),
+            jax.ShapeDtypeStruct((days, k // cells), jnp.float32),
         ),
-        in_specs=[vmem, vmem, vmem, hbm],
+        in_specs=[vmem, vmem, hbm],
         out_specs=(vmem, hbm, vmem),
         scratch_shapes=[
             pltpu.VMEM((k, k), jnp.float32),
@@ -210,8 +243,9 @@
             pltpu.SemaphoreType.DMA,
             pltpu.SemaphoreType.DMA((steps,)),
         ],
+        compiler_params=pltpu.CompilerParams(vmem_limit_bytes=VMEM_LIMIT),
         name="factor",
-    )(mine, theirs, cross, sketch)
+    )(mine, theirs, sketch)
 
 
 def swap(value, axis, bit):
@@ -219,64 +253,29 @@
     return lax.ppermute(value, axis, [(i, i ^ bit) for i in range(size)])
 
 
-def halve(days, place, bit):
-    groups, rows, k = days.shape
-    pairs = days.reshape(groups // 2, 2, rows, k)
-    own = (place // bit) % 2
-    return (
-        lax.dynamic_index_in_dim(pairs, own, 1, keepdims=False),
-        lax.dynamic_index_in_dim(pairs, 1 - own, 1, keepdims=False),
-    )
-
-
-def flat(gram, days):
-    groups, rows, k = days.shape
-    days = days.reshape(groups * rows, k)
-    return jnp.concatenate([gram] + [days[:, i : i + LANES] for i in range(0, k, LANES)], 0)
-
-
-def unflat(both, gram_rows, groups, rows, k):
-    count = groups * rows
-    days = [both[gram_rows + i * count : gram_rows + (i + 1) * count] for i in range(k // LANES)]
-    return both[:gram_rows], jnp.concatenate(days, 1).reshape(groups, rows, k)
-
-
 def local(sketch, slab):
     cells, groups = lax.axis_size("cell"), lax.axis_size("grp")
     place = lax.axis_index("grp")
-    gram, days = local_stats(sketch, slab)
-    k = gram.shape[0]
-    n = k // 2
-    top, low, square = gram[:n, :n], gram[n:, n:], gram[n:, :n]
-    row = lax.broadcasted_iota(jnp.int32, (n, n), 0)
-    col = lax.broadcasted_iota(jnp.int32, (n, n), 1)
-    packed = jnp.where(row >= col, top, low)
-    diagonal = jnp.sum(jnp.where(row == col, low, 0.0), axis=0, keepdims=True)
-    extra = jnp.broadcast_to(diagonal, (SUB, n))
-    halves = jnp.stack([jnp.concatenate([square, extra], 0), jnp.concatenate([packed, extra], 0)])
-    core = place % 2
-    kept = lax.dynamic_index_in_dim(halves, core, 0, keepdims=False)
-    sent = lax.dynamic_index_in_dim(halves, 1 - core, 0, keepdims=False)
-    days = days.reshape(groups, days.shape[0] // groups, k)
-    bit = 1
+    shared = sketch.shape[1] // 2 + SUB
+    kept, sent = local_stats(sketch, slab, groups)
+    both = kept + swap(sent, "grp", 1)
+    bit = 2
     while bit < groups:
-        days_kept, days_sent = halve(days, place, bit)
-        if bit == 1:
-            gram_kept, gram_sent = kept, sent
-        else:
-            gram_kept = gram_sent = kept
-        got = swap(flat(gram_sent, days_sent), "grp", bit)
-        both = flat(gram_kept, days_kept) + got
-        kept, days = unflat(both, gram_kept.shape[0], *days_kept.shape)
+        gram, days = both[:shared], both[shared:]
+        days = days.reshape(groups // (2 * bit), 2, -1, LANES)
+        own = (place // bit) % 2
+        kept_days = lax.dynamic_index_in_dim(days, own, 1, keepdims=False).reshape(-1, LANES)
+        sent_days = lax.dynamic_index_in_dim(days, 1 - own, 1, keepdims=False).reshape(-1, LANES)
+        got = swap(jnp.concatenate([gram, sent_days], 0), "grp", bit)
+        both = jnp.concatenate([gram, kept_days], 0) + got
         bit *= 2
     bit = 1
     while bit < cells:
         both = both + swap(both, "cell", bit)
         bit *= 2
-    kept, days = unflat(both, kept.shape[0], *days.shape)
-    theirs = swap(kept, "grp", 1)
-    r_factor, basis, projected = factor(kept, theirs, days[0], sketch, cells)
-    return r_factor, basis, projected
+    theirs = swap(both[:shared], "grp", 1)
+    r_factor, basis, projected = factor(both, theirs, sketch, cells)
+    return r_factor, basis, projected.T
 
 
 def solution(mesh):

time: 43.5 us -> 39.4 us (0.906)
  Pallas kernels: 18.8 us -> 16.4 us
  other arithmetic: 1.69 us -> 0.07 us
  waiting for transfers between devices: 10.4 us -> 11 us
  local copies, waits for them, and re-layouts: 3.02 us -> 2.58 us
    unnamed x4 -> x6, local copies, waits for them, and re-layouts: 0.63 us -> 2.54 us
    pallas_call x1, Pallas kernels: 15.6 us -> 13.8 us  [factor(): pl.pallas_call(functools.partial(factor_kernel, steps, cells), out_shape=...]
    pallas_call x1 -> x0, local copies, waits for them, and re-layouts: 1.44 us -> none  [factor(): pl.pallas_call(functools.partial(factor_kernel, steps, cells), out_shape=...]
    select_n x1 -> x0, other arithmetic: 0.94 us -> none  [local(): packed = jnp.where(row >= col, top, low)]
    dynamic_slice x1 -> x0, local copies, waits for them, and re-layouts: 0.89 us -> none  [halve(): lax.dynamic_index_in_dim(pairs, own, 1, keepdims=False)]
    concatenate x4 -> x1, other arithmetic: 0.63 us -> 0.01 us  [local(): got = swap(jnp.concatenate([gram, sent_days], 0), 'grp', bit)]
    ppermute x5, waiting for transfers between devices: 10.4 us -> 11 us  [swap(): return lax.ppermute(value, axis, [(i, i ^ bit) for i in range(size)])]
    pallas_call x1, Pallas kernels: 3.22 us -> 2.63 us  [local_stats(): pl.pallas_call(functools.partial(stats_kernel, steps, groups), out_shape=...]
  transfers between devices with their start and end apart: 5 -> 5, of which waited for: 5 -> 5; matrix products, arithmetic and copies ran while one was open for 1% -> 0% of each run, Pallas kernels for 0% -> 0%
where the time goes in v2:
time: 39.4 us; the launch traced here: 39.1 us
  Pallas kernels  16.4 us (42%)
  waiting for transfers between devices  11 us (28%)
  starting transfers between devices  8.3 us (21%)
  local copies, waits for them, and re-layouts  2.58 us (7%)
  between operations  0.71 us (2%)
    pallas_call x1, Pallas kernels, factor(): pl.pallas_call(functools.partial(factor_kernel, steps, cells), out_shape=...  13.8 us
    ppermute x5, waiting for transfers between devices, swap(): return lax.ppermute(value, axis, [(i, i ^ bit) for i in range(size)])  11 us
    ppermute x5, starting transfers between devices, swap(): return lax.ppermute(value, axis, [(i, i ^ bit) for i in range(size)])  8.3 us
    pallas_call x1, Pallas kernels, local_stats(): pl.pallas_call(functools.partial(stats_kernel, steps, groups), out_shape=...  2.63 us
    unnamed x6, local copies, waits for them, and re-layouts  2.54 us
  transfers between devices with their start and end apart: 5, of which 5 were waited for; matrix products, arithmetic and copies ran while one was open for 0% of the time, Pallas kernels for 0%

profile of v2, /device:TPU:0, one launch (start us, length us, event | category | flops | bytes accessed | tf_op | source)
XLA Modules:
  0.0 39.1 jit_solution(15698216788097071351)
XLA Ops:
  0.6 0.0 copy-start
  0.6 1.4 %copy-done = bf16[3072,256]{1,0:T(8,128)(2,1)S(1)} copy-done((bf16[3072,256]{1,0:T(8,128)(2,1)S(1)}, bf16[3072,256]{1,0:T(8,128)(2,1)}, u32[]{:S(2)}) %copy-start) | copy-done | bytes 1572888
  2.0 0.0 copy-start.2
  2.0 1.1 %copy-done.2 = bf16[3072,128]{1,0:T(8,128)(2,1)S(1)} copy-done((bf16[3072,128]{1,0:T(8,128)(2,1)S(1)}, bf16[3072,128]{1,0:T(8,128)(2,1)}, u32[]{:S(2)}) %copy-start.2) | copy-done | bytes 786456
  3.2 2.6 %local_stats.1 = (f32[264,128]{1,0:T(8,128)S(1)}, f32[264,128]{1,0:T(8,128)S(1)}) custom-call(bf16[3072,256]{1,0:T(8,128)(2,1)S(1)} %copy-done, bf16[3072,128]{1,0:T(8,128)(2,1)S(1)} %copy-done.2), custom_call_target="tpu_custom_call" | custom-call | tf_op jit(solution)/shard_map/local_stats/pallas_call | solution.py:77
  5.8 0.0 copy-start.1
  5.8 0.5 %collective-permute-start = (f32[264,128]{1,0:T(8,128)S(1)}, f32[264,128]{1,0:T(8,128)S(1)}, u32[]{:S(2)}, u32[]{:S(2)}) collective-permute-start(f32[264,128]{1,0:T(8,128)S(1)} %get-tuple-element.9), channel_id=1, source_target_pairs={{0,1},{1,0},{2,3},{3,2},{4,5},{5,4},{6,7},{7,6},{8,9},{9,8},{10,11... | collective-permute-start | bytes 405512 | tf_op jit(solution)/shard_map/ppermute | solution.py:253
  6.3 1.0 %collective-permute-done = f32[264,128]{1,0:T(8,128)S(1)} collective-permute-done((f32[264,128]{1,0:T(8,128)S(1)}, f32[264,128]{1,0:T(8,128)S(1)}, u32[]{:S(2)}, u32[]{:S(2)}) %collective-permute-start) | collective-permute-done | bytes 135200 | tf_op jit(solution)/shard_map/ppermute | solution.py:253
  7.4 2.9 %collective-permute-start.1 = (f32[200,128]{1,0:T(8,128)S(1)}, f32[200,128]{1,0:T(8,128)S(1)}, u32[]{:S(2)}, u32[]{:S(2)}) collective-permute-start(f32[200,128]{1,0:T(8,128)S(1)} %pad_maximum_fusion), channel_id=1, source_target_pairs={{0,2},{1,3},{2,0},{3,1},{4,6},{5,7},{6,4},{7,5},{8,10},{9,11},{10,... | collective-permute-start | bytes 307208 | tf_op jit(solution)/shard_map/ppermute | solution.py:253
  10.3 3.2 %collective-permute-done.1 = f32[200,128]{1,0:T(8,128)S(1)} collective-permute-done((f32[200,128]{1,0:T(8,128)S(1)}, f32[200,128]{1,0:T(8,128)S(1)}, u32[]{:S(2)}, u32[]{:S(2)}) %collective-permute-start.1) | collective-permute-done | bytes 102432 | tf_op jit(solution)/shard_map/ppermute | solution.py:253
  13.6 1.9 %collective-permute-start.2 = (f32[200,128]{1,0:T(8,128)S(1)}, f32[200,128]{1,0:T(8,128)S(1)}, u32[]{:S(2)}, u32[]{:S(2)}) collective-permute-start(f32[200,128]{1,0:T(8,128)S(1)} %fusion), channel_id=1, source_target_pairs={{0,4},{4,0},{8,12},{12,8},{1,5},{5,1},{9,13},{13,9},{2,6},{6,2},{1... | collective-permute-start | bytes 307208 | tf_op jit(solution)/shard_map/ppermute | solution.py:253
  15.4 2.8 %collective-permute-done.2 = f32[200,128]{1,0:T(8,128)S(1)} collective-permute-done((f32[200,128]{1,0:T(8,128)S(1)}, f32[200,128]{1,0:T(8,128)S(1)}, u32[]{:S(2)}, u32[]{:S(2)}) %collective-permute-start.2) | collective-permute-done | bytes 102432 | tf_op jit(solution)/shard_map/ppermute | solution.py:253
  18.3 2.9 %collective-permute-start.3 = (f32[200,128]{1,0:T(8,128)S(1)}, f32[200,128]{1,0:T(8,128)S(1)}, u32[]{:S(2)}, u32[]{:S(2)}) collective-permute-start(f32[200,128]{1,0:T(8,128)S(1)} %add.30), channel_id=1, source_target_pairs={{0,8},{4,12},{8,0},{12,4},{1,9},{5,13},{9,1},{13,5},{2,10},{6,14},... | collective-permute-start | bytes 307208 | tf_op jit(solution)/shard_map/ppermute | solution.py:253
  21.2 2.7 %collective-permute-done.3 = f32[200,128]{1,0:T(8,128)S(1)} collective-permute-done((f32[200,128]{1,0:T(8,128)S(1)}, f32[200,128]{1,0:T(8,128)S(1)}, u32[]{:S(2)}, u32[]{:S(2)}) %collective-permute-start.3) | collective-permute-done | bytes 102432 | tf_op jit(solution)/shard_map/ppermute | solution.py:253
  24.0 0.1 collective-permute-start.4
  24.0 1.2 %collective-permute-done.4.theirs_ref = f32[136,128]{1,0:T(8,128)S(1)} collective-permute-done((f32[136,128]{1,0:T(8,128)S(1)}, f32[136,128]{1,0:T(8,128)S(1)}, u32[]{:S(2)}, u32[]{:S(2)}) %collective-permute-start.4) | collective-permute-done | bytes 69664 | tf_op jit(solution)/shard_map/ppermute | solution.py:253
  25.3 0.0 copy-done.1
  25.3 13.8 %factor.1 = (f32[256,256]{1,0:T(8,128)}, bf16[3072,256]{1,0:T(8,128)(2,1)}, f32[32,64]{1,0:T(8,128)}) custom-call(f32[200,128]{1,0:T(8,128)S(1)} %add.31.mine_ref, f32[136,128]{1,0:T(8,128)S(1)} %collective-permute-done.4.theirs_ref, bf16[3072,256]{1,0:T(8,128)(2,1)S(1)} %copy-done.1), custom_call_target="tpu_custom_call" | custom-call | tf_op jit(solution)/shard_map/factor/pallas_call | solution.py:229
  (9 shorter events, 0.1 us)
Async XLA Ops:
  0.6 1.4 %copy-start = (bf16[3072,256]{1,0:T(8,128)(2,1)S(1)}, bf16[3072,256]{1,0:T(8,128)(2,1)}, u32[]{:S(2)}) copy-start(bf16[3072,256]{1,0:T(8,128)(2,1)} %sketch_hbm.3) | copy-start | bytes 4718596
  2.0 1.1 %copy-start.2 = (bf16[3072,128]{1,0:T(8,128)(2,1)S(1)}, bf16[3072,128]{1,0:T(8,128)(2,1)}, u32[]{:S(2)}) copy-start(bf16[3072,128]{1,0:T(8,128)(2,1)} %slab_hbm.1) | copy-start | bytes 2359300
  5.8 19.5 %copy-start.1 = (bf16[3072,256]{1,0:T(8,128)(2,1)S(1)}, bf16[3072,256]{1,0:T(8,128)(2,1)}, u32[]{:S(2)}) copy-start(bf16[3072,256]{1,0:T(8,128)(2,1)} %sketch_hbm.3) | copy-start | bytes 4718596
  5.8 1.5 %collective-permute-start = (f32[264,128]{1,0:T(8,128)S(1)}, f32[264,128]{1,0:T(8,128)S(1)}, u32[]{:S(2)}, u32[]{:S(2)}) collective-permute-start(f32[264,128]{1,0:T(8,128)S(1)} %get-tuple-element.9), channel_id=1, source_target_pairs={{0,1},{1,0},{2,3},{3,2},{4,5},{5,4},{6,7},{7,6},{8,9},{9,8},{10,11... | collective-permute-start | bytes 405512 | tf_op jit(solution)/shard_map/ppermute | solution.py:253
  7.4 6.1 %collective-permute-start.1 = (f32[200,128]{1,0:T(8,128)S(1)}, f32[200,128]{1,0:T(8,128)S(1)}, u32[]{:S(2)}, u32[]{:S(2)}) collective-permute-start(f32[200,128]{1,0:T(8,128)S(1)} %pad_maximum_fusion), channel_id=1, source_target_pairs={{0,2},{1,3},{2,0},{3,1},{4,6},{5,7},{6,4},{7,5},{8,10},{9,11},{10,... | collective-permute-start | bytes 307208 | tf_op jit(solution)/shard_map/ppermute | solution.py:253
  13.6 4.7 %collective-permute-start.2 = (f32[200,128]{1,0:T(8,128)S(1)}, f32[200,128]{1,0:T(8,128)S(1)}, u32[]{:S(2)}, u32[]{:S(2)}) collective-permute-start(f32[200,128]{1,0:T(8,128)S(1)} %fusion), channel_id=1, source_target_pairs={{0,4},{4,0},{8,12},{12,8},{1,5},{5,1},{9,13},{13,9},{2,6},{6,2},{1... | collective-permute-start | bytes 307208 | tf_op jit(solution)/shard_map/ppermute | solution.py:253
  18.3 5.6 %collective-permute-start.3 = (f32[200,128]{1,0:T(8,128)S(1)}, f32[200,128]{1,0:T(8,128)S(1)}, u32[]{:S(2)}, u32[]{:S(2)}) collective-permute-start(f32[200,128]{1,0:T(8,128)S(1)} %add.30), channel_id=1, source_target_pairs={{0,8},{4,12},{8,0},{12,4},{1,9},{5,13},{9,1},{13,5},{2,10},{6,14},... | collective-permute-start | bytes 307208 | tf_op jit(solution)/shard_map/ppermute | solution.py:253
  24.0 1.3 %collective-permute-start.4 = (f32[136,128]{1,0:T(8,128)S(1)}, f32[136,128]{1,0:T(8,128)S(1)}, u32[]{:S(2)}, u32[]{:S(2)}) collective-permute-start(f32[136,128]{1,0:T(8,128)S(1)} %slice.14), channel_id=1, source_target_pairs={{0,1},{1,0},{2,3},{3,2},{4,5},{5,4},{6,7},{7,6},{8,9},{9,8},{10,11... | collective-permute-start | bytes 208904 | tf_op jit(solution)/shard_map/ppermute | solution.py:253

commit v3 on v2

--- a/solution.py
+++ b/solution.py
@@ -9,6 +9,7 @@
 
 SUB, LANES = 8, 128
 VMEM_LIMIT = 24 * 2**20
+STATS_LIMIT = 56 * 10**6
 HIGHEST = lax.Precision.HIGHEST
 
 
@@ -70,7 +71,7 @@
 def local_stats(sketch, slab, groups):
     rows, k = sketch.shape
     days = slab.shape[1]
-    steps = chunks_of(rows, 6)
+    steps = chunks_of(rows, 3)
     hbm = pl.BlockSpec(memory_space=pltpu.HBM)
     vmem = pl.BlockSpec(memory_space=pltpu.VMEM)
     out = jax.ShapeDtypeStruct((k // 2 + SUB + days // 2 * (k // LANES), LANES), jnp.float32)
@@ -86,70 +87,16 @@
             pltpu.VMEM((days, k), jnp.float32),
             pltpu.SemaphoreType.DMA((2, steps)),
         ],
-        compiler_params=pltpu.CompilerParams(vmem_limit_bytes=VMEM_LIMIT),
+        compiler_params=pltpu.CompilerParams(vmem_limit_bytes=STATS_LIMIT),
         name="local_stats",
     )(sketch, slab)
 
 
-def eliminate(a_ref, r_ref, x_ref):
-    k = a_ref.shape[0]
-    halves = k // LANES
-    shape = (SUB, LANES)
-    sub = lax.broadcasted_iota(jnp.int32, shape, 0)
-    lane = lax.broadcasted_iota(jnp.int32, shape, 1)
-
-    def load(panel):
-        rows = pl.ds(panel * SUB, SUB)
-        return [a_ref[rows, pl.ds(h * LANES, LANES)] for h in range(halves)]
-
-    def row_of(v, i):
-        return jnp.broadcast_to(v[i : i + 1, :], shape)
-
-    def column_of(v, i):
-        return jnp.broadcast_to(v[:, i : i + 1], shape)
-
-    for panel in range(k // SUB):
-        half, first = divmod(panel * SUB, LANES)
-        block = load(panel)
-        cols = [column_of(block[half], first + i) for i in range(SUB)]
-        saved = [jnp.zeros(shape, jnp.float32)] * halves
-        scale = jnp.zeros(shape, jnp.float32)
-        for i in range(SUB):
-            here = sub == i
-            pivot = row_of(cols[i], i)
-            inverse = 1.0 / pivot
-            root = lax.rsqrt(pivot)
-            scale = jnp.where(here, root, scale)
-            saved = [jnp.where(here, b, s) for b, s in zip(block, saved)]
-            unit = jnp.where(here, 1.0, 0.0)
-            block[half] = jnp.where(lane == first + i, unit, block[half])
-
-            def step(v):
-                row = row_of(v, i)
-                return jnp.where(here, row * inverse, v - (cols[i] * row) * inverse)
-
-            for j in range(i + 1, SUB):
-                cols[j] = step(cols[j])
-            block = [step(b) for b in block]
-        rows = pl.ds(panel * SUB, SUB)
-        for h in range(halves):
-            at = pl.ds(h * LANES, LANES)
-            ahead = lane + h * LANES - (sub + panel * SUB)
-            z = saved[h] * scale
-            r_ref[rows, at] = jnp.where(ahead >= 0, z, 0.0)
-            x_ref[rows, at] = jnp.where(ahead < 0, z, jnp.where(ahead == 0, scale, 0.0))
-        pivots = [[row_of(b, i) for b in block] for i in range(SUB)]
-        inside = (lane >= first) & (lane < first + SUB)
-        for other in range(panel + 1, k // SUB):
-            target = load(other)
-            coefs = [column_of(target[half], first + i) for i in range(SUB)]
-            target[half] = jnp.where(inside, 0.0, target[half])
-            rows = pl.ds(other * SUB, SUB)
-            for h in range(halves):
-                total = coefs[0] * pivots[0][h]
-                for i in range(1, SUB):
-                    total = total + coefs[i] * pivots[i][h]
-                a_ref[rows, pl.ds(h * LANES, LANES)] = target[h] - total
+def tree_sum(terms):
+    while len(terms) > 1:
+        odd = terms[len(terms) & ~1 :]
+        terms = [x + y for x, y in zip(terms[::2], terms[1::2])] + odd
+    return terms[0]
 
 
 def split3(v):
@@ -160,49 +107,161 @@
     return high, middle, low
 
 
+def eliminate(a_ref, one_ref, scale, unscale, r_ref, x_ref):
+    k = a_ref.shape[0]
+    halves, panels = k // LANES, k // SUB
+    shape = (SUB, LANES)
+    sub = lax.broadcasted_iota(jnp.int32, shape, 0)
+    lane = lax.broadcasted_iota(jnp.int32, shape, 1)
+    here = [sub == i for i in range(SUB)]
+    one = one_ref[...]
+
+    def rows_of(panel):
+        return pl.ds(panel * SUB, SUB)
+
+    def lanes_of(half):
+        return pl.ds(half * LANES, LANES)
+
+    def load(panel):
+        return [a_ref[rows_of(panel), lanes_of(h)] for h in range(halves)]
+
+    def row_of(v, i):
+        return jnp.broadcast_to(v[i : i + 1, :], shape)
+
+    def column_of(v, i):
+        return jnp.broadcast_to(v[:, i : i + 1], shape)
+
+    def follow(target, panel, pivots):
+        half, first = divmod(panel * SUB, LANES)
+        coefs = [column_of(target[half], first + i) for i in range(SUB)]
+        inside = (lane >= first) & (lane < first + SUB)
+        rest = list(target)
+        rest[half] = jnp.where(inside, 0.0, rest[half])
+        return [
+            rest[h] - tree_sum([coefs[i] * pivots[i][h] for i in range(SUB)]) for h in range(halves)
+        ]
+
+    def solve(panel, block):
+        half, first = divmod(panel * SUB, LANES)
+        block = list(block)
+        cols = [column_of(block[half], first + i) * one for i in range(SUB)]
+        saved = [jnp.zeros(shape, jnp.float32)] * halves
+        roots = jnp.zeros(shape, jnp.float32)
+        for i in range(0, SUB, 2):
+            upper, lower = here[i], here[i + 1]
+            both = upper | lower
+            p, q, r = row_of(cols[i], i), row_of(cols[i + 1], i), row_of(cols[i + 1], i + 1)
+            det = p * r - q * q
+            inverse = 1.0 / det
+            over = 1.0 / p
+            roots = jnp.where(
+                both, jnp.where(upper, lax.rsqrt(p), lax.rsqrt(det * over)), roots
+            )
+            ratio = jnp.where(lower, q * over, 0.0)
+            for h in range(halves):
+                z = block[h] - ratio * row_of(block[h], i)
+                if h == half:
+                    z = jnp.where((lane == first + i) & lower, -ratio, z)
+                saved[h] = jnp.where(both, z, saved[h])
+            left = jnp.where(upper, -1.0, jnp.where(lower, 0.0, cols[i]))
+            right = jnp.where(upper, 0.0, jnp.where(lower, -1.0, cols[i + 1]))
+            on_upper = left * r - right * q
+            on_lower = right * p - left * q
+
+            def step(v):
+                change = row_of(v, i) * on_upper + row_of(v, i + 1) * on_lower
+                return jnp.where(both, 0.0, v) - change * inverse
+
+            unit = jnp.where(
+                lane == first + i, jnp.where(upper, 1.0, 0.0), jnp.where(lower, 1.0, 0.0)
+            )
+            pair = (lane == first + i) | (lane == first + i + 1)
+            block[half] = jnp.where(pair, unit, block[half])
+            cols = [step(c) if j > i + 1 else c for j, c in enumerate(cols)]
+            block = [step(v) for v in block]
+        for h in range(halves):
+            ahead = lane + h * LANES - (sub + panel * SUB)
+            z = saved[h] * roots
+            inverse_part = jnp.where(ahead < 0, z, jnp.where(ahead == 0, roots, 0.0))
+            r_ref[rows_of(panel), lanes_of(h)] = jnp.where(ahead >= 0, z, 0.0) * unscale[h]
+            x_ref[rows_of(panel), lanes_of(h)] = inverse_part * scale[h]
+        return block
+
+    per = 4
+    size = per * SUB
+    blocks = k // size
+    lanes_all = lax.broadcasted_iota(jnp.int32, (size, k), 1)
+    panel_all = lax.broadcasted_iota(jnp.int32, (size, k), 0) // SUB
+    ahead_block = None
+    for number in range(blocks):
+        befores, afters = [], []
+        for panel in range(number * per, (number + 1) * per):
+            before = load(panel) if ahead_block is None else ahead_block
+            after = solve(panel, before)
+            befores.append(jnp.concatenate(before, 1))
+            afters.append(jnp.concatenate(after, 1))
+            pivots = [[row_of(v, i) for v in after] for i in range(SUB)]
+            for other in range(panel + 1, min((number + 2) * per, panels)):
+                target = follow(load(other), panel, pivots)
+                if other == panel + 1:
+                    ahead_block = target
+                    continue
+                for h in range(halves):
+                    a_ref[rows_of(other), lanes_of(h)] = target[h]
+        if number + 2 >= blocks:
+            continue
+        low = number * size
+        top = (number + 2) * size
+        base = top // LANES * LANES
+        lhs = split3(jnp.concatenate(befores, 0)[:, base:])
+        later = (lanes_all < low + size) & (lanes_all >= low + (panel_all + 1) * SUB)
+        rhs = split3(jnp.where(later, 0.0, jnp.concatenate(afters, 0)))
+        change = lax.dot_general(
+            jnp.concatenate([lhs[i] for i in (0, 0, 1, 0, 2, 1)], 0),
+            jnp.concatenate([rhs[i] for i in (0, 1, 0, 2, 0, 1)], 0),
+            (((0,), (0,)), ((), ())),
+            preferred_element_type=jnp.float32,
+        )[top - base :]
+        lanes = lax.broadcasted_iota(jnp.int32, (k - top, k), 1)
+        inside = (lanes >= low) & (lanes < low + size)
+        a_ref[top:k, :] = jnp.where(inside, 0.0, a_ref[top:k, :]) - change
+
+
 def factor_kernel(
-    steps, cells, mine_ref, theirs_ref, sketch_hbm, r_ref, basis_hbm, proj_ref,
-    a_ref, x_ref, sketch, basis, sem_in, sems,
+    steps, cells, mine_ref, theirs_ref, sketch_hbm, r_hbm, basis_hbm, proj_hbm,
+    a_ref, one_ref, r_ref, x_ref, proj_ref, sketch, basis, sem_in, sem_r, sem_proj, sems,
 ):
     copy_in = pltpu.make_async_copy(sketch_hbm, sketch, sem_in)
     copy_in.start()
     k = a_ref.shape[0]
     n = k // 2
-    core = lax.axis_index("grp") % 2
-    first = core == 0
+    one_ref[...] = jnp.ones_like(one_ref)
+    first = lax.axis_index("grp") % 2 == 0
     square = jnp.where(first, mine_ref[0:n, :], theirs_ref[0:n, :])
     packed = jnp.where(first, theirs_ref[0:n, :], mine_ref[0:n, :])
-    diagonal = jnp.where(first, theirs_ref[n : n + 1, :], mine_ref[n : n + 1, :])
-    turned = packed.T
     row = lax.broadcasted_iota(jnp.int32, (n, n), 0)
     col = lax.broadcasted_iota(jnp.int32, (n, n), 1)
+    norms = [
+        jnp.sum(jnp.where(row == col, packed, 0.0), axis=0, keepdims=True),
+        mine_ref[n : n + 1, :],
+    ]
+    scale = [lax.rsqrt(v) for v in norms]
+    unscale = [v * s for v, s in zip(norms, scale)]
+    turned = jnp.where(row >= col, packed * scale[0], packed * scale[1]).T
+    turned = jnp.where(row <= col, turned * scale[0], turned * scale[1])
+    packed = turned.T
     a_ref[0:n, 0:n] = jnp.where(row >= col, packed, turned)
-    a_ref[0:n, n:k] = square.T
-    a_ref[n:k, 0:n] = square
-    a_ref[n:k, n:k] = jnp.where(
-        row < col, packed, jnp.where(row > col, turned, jnp.broadcast_to(diagonal, (n, n)))
-    )
-    eliminate(a_ref, r_ref, x_ref)
-    count = k // cells
-    start = pl.multiple_of(lax.axis_index("cell") * count, count)
-    own_rows = pl.ds(start, count)
-    days = proj_ref.shape[0]
-    total = None
-    for h in range(k // LANES):
-        at = n + SUB + h * days
-        term = lax.dot_general(
-            mine_ref[at : at + days, :],
-            x_ref[own_rows, h * LANES : (h + 1) * LANES],
-            (((1,), (1,)), ((), ())),
-            precision=HIGHEST,
-            preferred_element_type=jnp.float32,
-        )
-        total = term if total is None else total + term
-    proj_ref[...] = total
+    a_ref[n:k, n:k] = jnp.where(row < col, packed, jnp.where(row > col, turned, 1.0))
+    square = (square * scale[0]).T * scale[1]
+    a_ref[0:n, n:k] = square
+    a_ref[n:k, 0:n] = square.T
+    eliminate(a_ref, one_ref, scale, unscale, r_ref, x_ref)
+    copy_r = pltpu.make_async_copy(r_ref, r_hbm, sem_r)
+    copy_r.start()
+    copies = [copy_r]
     parts = split3(x_ref[...])
     copy_in.wait()
     size = sketch.shape[0] // steps
-    copies = []
     for step in range(steps):
         rows = pl.ds(step * size, size)
         piece = sketch[rows, :]
@@ -214,6 +273,26 @@
             total = term if total is None else total + term
         basis[rows, :] = total.astype(basis.dtype)
         copy = pltpu.make_async_copy(basis.at[rows], basis_hbm.at[rows], sems.at[step])
+        copy.start()
+        copies.append(copy)
+        if step:
+            continue
+        count = k // cells
+        own_rows = pl.ds(pl.multiple_of(lax.axis_index("cell") * count, count), count)
+        days = proj_ref.shape[0]
+        total = None
+        for h in range(k // LANES):
+            at = n + SUB + h * days
+            term = lax.dot_general(
+                mine_ref[at : at + days, :],
+                x_ref[own_rows, h * LANES : (h + 1) * LANES],
+                (((1,), (1,)), ((), ())),
+                precision=HIGHEST,
+                preferred_element_type=jnp.float32,
+            )
+            total = term if total is None else total + term
+        proj_ref[...] = total
+        copy = pltpu.make_async_copy(proj_ref, proj_hbm, sem_proj)
         copy.start()
         copies.append(copy)
     for copy in copies:
@@ -234,12 +313,17 @@
             jax.ShapeDtypeStruct((days, k // cells), jnp.float32),
         ),
         in_specs=[vmem, vmem, hbm],
-        out_specs=(vmem, hbm, vmem),
+        out_specs=(hbm, hbm, hbm),
         scratch_shapes=[
             pltpu.VMEM((k, k), jnp.float32),
+            pltpu.VMEM((SUB, LANES), jnp.float32),
             pltpu.VMEM((k, k), jnp.float32),
+            pltpu.VMEM((k, k), jnp.float32),
+            pltpu.VMEM((days, k // cells), jnp.float32),
             pltpu.VMEM((rows, k), sketch.dtype),
             pltpu.VMEM((rows, k), jnp.bfloat16),
+            pltpu.SemaphoreType.DMA,
+            pltpu.SemaphoreType.DMA,
             pltpu.SemaphoreType.DMA,
             pltpu.SemaphoreType.DMA((steps,)),
         ],

time: 39.4 us -> 30.4 us (0.77)
  Pallas kernels: 16.4 us -> 10 us
  local copies, waits for them, and re-layouts: 2.58 us -> 0.04 us
    pallas_call x1, Pallas kernels: 13.8 us -> 7.7 us  [factor(): pl.pallas_call(functools.partial(factor_kernel, steps, cells), out_shape=...]
    unnamed x6 -> x2, local copies, waits for them, and re-layouts: 2.54 us -> 0.01 us
where the time goes in v3:
time: 30.4 us; the launch traced here: 30.1 us
  waiting for transfers between devices  11 us (36%)
  Pallas kernels  10 us (33%)
  starting transfers between devices  8.29 us (27%)
  between operations  0.7 us (2%)
    ppermute x5, waiting for transfers between devices, swap(): return lax.ppermute(value, axis, [(i, i ^ bit) for i in range(size)])  11 us
    ppermute x5, starting transfers between devices, swap(): return lax.ppermute(value, axis, [(i, i ^ bit) for i in range(size)])  8.29 us
    pallas_call x1, Pallas kernels, factor(): pl.pallas_call(functools.partial(factor_kernel, steps, cells), out_shape=...  7.7 us
    pallas_call x1, Pallas kernels, local_stats(): pl.pallas_call(functools.partial(stats_kernel, steps, groups), out_shape=...  2.35 us
  transfers between devices with their start and end apart: 5, of which 5 were waited for; matrix products, arithmetic and copies ran while one was open for 0% of the time, Pallas kernels for 0%

profile of v3, /device:TPU:0, one launch (start us, length us, event | category | flops | bytes accessed | tf_op | source)
XLA Modules:
  0.0 30.1 jit_solution(5940802675563787439)
XLA Ops:
  0.6 2.3 %local_stats.1 = (f32[264,128]{1,0:T(8,128)S(1)}, f32[264,128]{1,0:T(8,128)S(1)}) custom-call(bf16[3072,256]{1,0:T(8,128)(2,1)} %sketch_hbm.3, bf16[3072,128]{1,0:T(8,128)(2,1)} %slab_hbm.1), custom_call_target="tpu_custom_call" | custom-call | tf_op jit(solution)/shard_map/local_stats/pallas_call | solution.py:78
  3.0 0.0 copy-start
  3.0 0.5 %collective-permute-start = (f32[264,128]{1,0:T(8,128)S(1)}, f32[264,128]{1,0:T(8,128)S(1)}, u32[]{:S(2)}, u32[]{:S(2)}) collective-permute-start(f32[264,128]{1,0:T(8,128)S(1)} %get-tuple-element.9), channel_id=1, source_target_pairs={{0,1},{1,0},{2,3},{3,2},{4,5},{5,4},{6,7},{7,6},{8,9},{9,8},{10,11... | collective-permute-start | bytes 405512 | tf_op jit(solution)/shard_map/ppermute | solution.py:337
  3.5 1.0 %collective-permute-done = f32[264,128]{1,0:T(8,128)S(1)} collective-permute-done((f32[264,128]{1,0:T(8,128)S(1)}, f32[264,128]{1,0:T(8,128)S(1)}, u32[]{:S(2)}, u32[]{:S(2)}) %collective-permute-start) | collective-permute-done | bytes 135200 | tf_op jit(solution)/shard_map/ppermute | solution.py:337
  4.6 2.9 %collective-permute-start.1 = (f32[200,128]{1,0:T(8,128)S(1)}, f32[200,128]{1,0:T(8,128)S(1)}, u32[]{:S(2)}, u32[]{:S(2)}) collective-permute-start(f32[200,128]{1,0:T(8,128)S(1)} %pad_maximum_fusion), channel_id=1, source_target_pairs={{0,2},{1,3},{2,0},{3,1},{4,6},{5,7},{6,4},{7,5},{8,10},{9,11},{10,... | collective-permute-start | bytes 307208 | tf_op jit(solution)/shard_map/ppermute | solution.py:337
  7.5 3.2 %collective-permute-done.1 = f32[200,128]{1,0:T(8,128)S(1)} collective-permute-done((f32[200,128]{1,0:T(8,128)S(1)}, f32[200,128]{1,0:T(8,128)S(1)}, u32[]{:S(2)}, u32[]{:S(2)}) %collective-permute-start.1) | collective-permute-done | bytes 102432 | tf_op jit(solution)/shard_map/ppermute | solution.py:337
  10.7 1.9 %collective-permute-start.2 = (f32[200,128]{1,0:T(8,128)S(1)}, f32[200,128]{1,0:T(8,128)S(1)}, u32[]{:S(2)}, u32[]{:S(2)}) collective-permute-start(f32[200,128]{1,0:T(8,128)S(1)} %fusion), channel_id=1, source_target_pairs={{0,4},{4,0},{8,12},{12,8},{1,5},{5,1},{9,13},{13,9},{2,6},{6,2},{1... | collective-permute-start | bytes 307208 | tf_op jit(solution)/shard_map/ppermute | solution.py:337
  12.6 2.8 %collective-permute-done.2 = f32[200,128]{1,0:T(8,128)S(1)} collective-permute-done((f32[200,128]{1,0:T(8,128)S(1)}, f32[200,128]{1,0:T(8,128)S(1)}, u32[]{:S(2)}, u32[]{:S(2)}) %collective-permute-start.2) | collective-permute-done | bytes 102432 | tf_op jit(solution)/shard_map/ppermute | solution.py:337
  15.5 2.9 %collective-permute-start.3 = (f32[200,128]{1,0:T(8,128)S(1)}, f32[200,128]{1,0:T(8,128)S(1)}, u32[]{:S(2)}, u32[]{:S(2)}) collective-permute-start(f32[200,128]{1,0:T(8,128)S(1)} %add.30), channel_id=1, source_target_pairs={{0,8},{4,12},{8,0},{12,4},{1,9},{5,13},{9,1},{13,5},{2,10},{6,14},... | collective-permute-start | bytes 307208 | tf_op jit(solution)/shard_map/ppermute | solution.py:337
  18.4 2.7 %collective-permute-done.3 = f32[200,128]{1,0:T(8,128)S(1)} collective-permute-done((f32[200,128]{1,0:T(8,128)S(1)}, f32[200,128]{1,0:T(8,128)S(1)}, u32[]{:S(2)}, u32[]{:S(2)}) %collective-permute-start.3) | collective-permute-done | bytes 102432 | tf_op jit(solution)/shard_map/ppermute | solution.py:337
  21.1 0.1 collective-permute-start.4
  21.2 1.2 %collective-permute-done.4.theirs_ref = f32[136,128]{1,0:T(8,128)S(1)} collective-permute-done((f32[136,128]{1,0:T(8,128)S(1)}, f32[136,128]{1,0:T(8,128)S(1)}, u32[]{:S(2)}, u32[]{:S(2)}) %collective-permute-start.4) | collective-permute-done | bytes 69664 | tf_op jit(solution)/shard_map/ppermute | solution.py:337
  22.4 0.0 copy-done
  22.4 7.7 %factor.1 = (f32[256,256]{1,0:T(8,128)}, bf16[3072,256]{1,0:T(8,128)(2,1)}, f32[32,64]{1,0:T(8,128)}) custom-call(f32[200,128]{1,0:T(8,128)S(1)} %add.31.mine_ref, f32[136,128]{1,0:T(8,128)S(1)} %collective-permute-done.4.theirs_ref, bf16[3072,256]{1,0:T(8,128)(2,1)S(1)} %copy-done), custom_call_target="tpu_custom_call" | custom-call | tf_op jit(solution)/shard_map/factor/pallas_call | solution.py:308
  (9 shorter events, 0.1 us)
Async XLA Ops:
  3.0 19.5 %copy-start = (bf16[3072,256]{1,0:T(8,128)(2,1)S(1)}, bf16[3072,256]{1,0:T(8,128)(2,1)}, u32[]{:S(2)}) copy-start(bf16[3072,256]{1,0:T(8,128)(2,1)} %sketch_hbm.3) | copy-start | bytes 4718596
  3.0 1.5 %collective-permute-start = (f32[264,128]{1,0:T(8,128)S(1)}, f32[264,128]{1,0:T(8,128)S(1)}, u32[]{:S(2)}, u32[]{:S(2)}) collective-permute-start(f32[264,128]{1,0:T(8,128)S(1)} %get-tuple-element.9), channel_id=1, source_target_pairs={{0,1},{1,0},{2,3},{3,2},{4,5},{5,4},{6,7},{7,6},{8,9},{9,8},{10,11... | collective-permute-start | bytes 405512 | tf_op jit(solution)/shard_map/ppermute | solution.py:337
  4.6 6.1 %collective-permute-start.1 = (f32[200,128]{1,0:T(8,128)S(1)}, f32[200,128]{1,0:T(8,128)S(1)}, u32[]{:S(2)}, u32[]{:S(2)}) collective-permute-start(f32[200,128]{1,0:T(8,128)S(1)} %pad_maximum_fusion), channel_id=1, source_target_pairs={{0,2},{1,3},{2,0},{3,1},{4,6},{5,7},{6,4},{7,5},{8,10},{9,11},{10,... | collective-permute-start | bytes 307208 | tf_op jit(solution)/shard_map/ppermute | solution.py:337
  10.7 4.7 %collective-permute-start.2 = (f32[200,128]{1,0:T(8,128)S(1)}, f32[200,128]{1,0:T(8,128)S(1)}, u32[]{:S(2)}, u32[]{:S(2)}) collective-permute-start(f32[200,128]{1,0:T(8,128)S(1)} %fusion), channel_id=1, source_target_pairs={{0,4},{4,0},{8,12},{12,8},{1,5},{5,1},{9,13},{13,9},{2,6},{6,2},{1... | collective-permute-start | bytes 307208 | tf_op jit(solution)/shard_map/ppermute | solution.py:337
  15.5 5.6 %collective-permute-start.3 = (f32[200,128]{1,0:T(8,128)S(1)}, f32[200,128]{1,0:T(8,128)S(1)}, u32[]{:S(2)}, u32[]{:S(2)}) collective-permute-start(f32[200,128]{1,0:T(8,128)S(1)} %add.30), channel_id=1, source_target_pairs={{0,8},{4,12},{8,0},{12,4},{1,9},{5,13},{9,1},{13,5},{2,10},{6,14},... | collective-permute-start | bytes 307208 | tf_op jit(solution)/shard_map/ppermute | solution.py:337
  21.1 1.3 %collective-permute-start.4 = (f32[136,128]{1,0:T(8,128)S(1)}, f32[136,128]{1,0:T(8,128)S(1)}, u32[]{:S(2)}, u32[]{:S(2)}) collective-permute-start(f32[136,128]{1,0:T(8,128)S(1)} %slice.14), channel_id=1, source_target_pairs={{0,1},{1,0},{2,3},{3,2},{4,5},{5,4},{6,7},{7,6},{8,9},{9,8},{10,11... | collective-permute-start | bytes 208904 | tf_op jit(solution)/shard_map/ppermute | solution.py:337

commit v4 on v3

--- a/solution.py
+++ b/solution.py
@@ -51,11 +51,13 @@
     col = lax.broadcasted_iota(jnp.int32, (n, n), 1)
     square, top, low = gram_ref[n:k, 0:n], gram_ref[0:n, 0:n], gram_ref[n:k, n:k]
     packed = jnp.where(row >= col, top, low)
-    diagonal = jnp.sum(jnp.where(row == col, low, 0.0), axis=0, keepdims=True)
+    norms = [jnp.sum(jnp.where(row == col, v, 0.0), axis=0, keepdims=True) for v in (top, low)]
+    tile = lax.broadcasted_iota(jnp.int32, (SUB, n), 0)
+    diagonal = jnp.where(tile == 0, norms[0], jnp.where(tile == 1, norms[1], 0.0))
     kept_ref[0:n, :] = jnp.where(first, square, packed)
     sent_ref[0:n, :] = jnp.where(first, packed, square)
     for ref in (kept_ref, sent_ref):
-        ref[n : n + SUB, :] = jnp.broadcast_to(diagonal, (SUB, n))
+        ref[n : n + SUB, :] = diagonal
     count = cross_ref.shape[0] // groups
     at = n + SUB
     for pair in range(groups // 2):
@@ -241,20 +243,17 @@
     packed = jnp.where(first, theirs_ref[0:n, :], mine_ref[0:n, :])
     row = lax.broadcasted_iota(jnp.int32, (n, n), 0)
     col = lax.broadcasted_iota(jnp.int32, (n, n), 1)
-    norms = [
-        jnp.sum(jnp.where(row == col, packed, 0.0), axis=0, keepdims=True),
-        mine_ref[n : n + 1, :],
-    ]
+    norms = [mine_ref[n + i : n + i + 1, :] for i in range(2)]
     scale = [lax.rsqrt(v) for v in norms]
     unscale = [v * s for v, s in zip(norms, scale)]
-    turned = jnp.where(row >= col, packed * scale[0], packed * scale[1]).T
-    turned = jnp.where(row <= col, turned * scale[0], turned * scale[1])
-    packed = turned.T
-    a_ref[0:n, 0:n] = jnp.where(row >= col, packed, turned)
-    a_ref[n:k, n:k] = jnp.where(row < col, packed, jnp.where(row > col, turned, 1.0))
-    square = (square * scale[0]).T * scale[1]
-    a_ref[0:n, n:k] = square
-    a_ref[n:k, 0:n] = square.T
+    across = [jnp.broadcast_to(s, (n, n)) for s in scale]
+    down = [s.T for s in across]
+    turned = packed.T
+    a_ref[0:n, 0:n] = jnp.where(row >= col, packed, turned) * across[0] * down[0]
+    below = jnp.where(row < col, packed, turned) * across[1] * down[1]
+    a_ref[n:k, n:k] = jnp.where(row == col, 1.0, below)
+    a_ref[0:n, n:k] = square.T * across[1] * down[0]
+    a_ref[n:k, 0:n] = square * across[0] * down[1]
     eliminate(a_ref, one_ref, scale, unscale, r_ref, x_ref)
     copy_r = pltpu.make_async_copy(r_ref, r_hbm, sem_r)
     copy_r.start()

time: 30.4 us -> 30.3 us (level)
  no operation moved by 1% of the time
where the time goes in v4:
time: 30.3 us; the launch traced here: 30 us
  waiting for transfers between devices  11 us (36%)
  Pallas kernels  9.91 us (33%)
  starting transfers between devices  8.29 us (27%)
  between operations  0.7 us (2%)
    ppermute x5, waiting for transfers between devices, swap(): return lax.ppermute(value, axis, [(i, i ^ bit) for i in range(size)])  11 us
    ppermute x5, starting transfers between devices, swap(): return lax.ppermute(value, axis, [(i, i ^ bit) for i in range(size)])  8.29 us
    pallas_call x1, Pallas kernels, factor(): pl.pallas_call(functools.partial(factor_kernel, steps, cells), out_shape=...  7.56 us
    pallas_call x1, Pallas kernels, local_stats(): pl.pallas_call(functools.partial(stats_kernel, steps, groups), out_shape=...  2.35 us
  transfers between devices with their start and end apart: 5, of which 5 were waited for; matrix products, arithmetic and copies ran while one was open for 0% of the time, Pallas kernels for 0%

profile of v4, /device:TPU:0, one launch (start us, length us, event | category | flops | bytes accessed | tf_op | source)
XLA Modules:
  0.0 30.0 jit_solution(1585582691970889832)
XLA Ops:
  0.6 2.3 %local_stats.1 = (f32[264,128]{1,0:T(8,128)S(1)}, f32[264,128]{1,0:T(8,128)S(1)}) custom-call(bf16[3072,256]{1,0:T(8,128)(2,1)} %sketch_hbm.3, bf16[3072,128]{1,0:T(8,128)(2,1)} %slab_hbm.1), custom_call_target="tpu_custom_call" | custom-call | tf_op jit(solution)/shard_map/local_stats/pallas_call | solution.py:80
  3.0 0.0 copy-start
  3.0 0.5 %collective-permute-start = (f32[264,128]{1,0:T(8,128)S(1)}, f32[264,128]{1,0:T(8,128)S(1)}, u32[]{:S(2)}, u32[]{:S(2)}) collective-permute-start(f32[264,128]{1,0:T(8,128)S(1)} %get-tuple-element.9), channel_id=1, source_target_pairs={{0,1},{1,0},{2,3},{3,2},{4,5},{5,4},{6,7},{7,6},{8,9},{9,8},{10,11... | collective-permute-start | bytes 405512 | tf_op jit(solution)/shard_map/ppermute | solution.py:336
  3.5 1.0 %collective-permute-done = f32[264,128]{1,0:T(8,128)S(1)} collective-permute-done((f32[264,128]{1,0:T(8,128)S(1)}, f32[264,128]{1,0:T(8,128)S(1)}, u32[]{:S(2)}, u32[]{:S(2)}) %collective-permute-start) | collective-permute-done | bytes 135200 | tf_op jit(solution)/shard_map/ppermute | solution.py:336
  4.6 2.9 %collective-permute-start.1 = (f32[200,128]{1,0:T(8,128)S(1)}, f32[200,128]{1,0:T(8,128)S(1)}, u32[]{:S(2)}, u32[]{:S(2)}) collective-permute-start(f32[200,128]{1,0:T(8,128)S(1)} %pad_maximum_fusion), channel_id=1, source_target_pairs={{0,2},{1,3},{2,0},{3,1},{4,6},{5,7},{6,4},{7,5},{8,10},{9,11},{10,... | collective-permute-start | bytes 307208 | tf_op jit(solution)/shard_map/ppermute | solution.py:336
  7.5 3.2 %collective-permute-done.1 = f32[200,128]{1,0:T(8,128)S(1)} collective-permute-done((f32[200,128]{1,0:T(8,128)S(1)}, f32[200,128]{1,0:T(8,128)S(1)}, u32[]{:S(2)}, u32[]{:S(2)}) %collective-permute-start.1) | collective-permute-done | bytes 102432 | tf_op jit(solution)/shard_map/ppermute | solution.py:336
  10.7 1.9 %collective-permute-start.2 = (f32[200,128]{1,0:T(8,128)S(1)}, f32[200,128]{1,0:T(8,128)S(1)}, u32[]{:S(2)}, u32[]{:S(2)}) collective-permute-start(f32[200,128]{1,0:T(8,128)S(1)} %fusion), channel_id=1, source_target_pairs={{0,4},{4,0},{8,12},{12,8},{1,5},{5,1},{9,13},{13,9},{2,6},{6,2},{1... | collective-permute-start | bytes 307208 | tf_op jit(solution)/shard_map/ppermute | solution.py:336
  12.6 2.8 %collective-permute-done.2 = f32[200,128]{1,0:T(8,128)S(1)} collective-permute-done((f32[200,128]{1,0:T(8,128)S(1)}, f32[200,128]{1,0:T(8,128)S(1)}, u32[]{:S(2)}, u32[]{:S(2)}) %collective-permute-start.2) | collective-permute-done | bytes 102432 | tf_op jit(solution)/shard_map/ppermute | solution.py:336
  15.5 2.9 %collective-permute-start.3 = (f32[200,128]{1,0:T(8,128)S(1)}, f32[200,128]{1,0:T(8,128)S(1)}, u32[]{:S(2)}, u32[]{:S(2)}) collective-permute-start(f32[200,128]{1,0:T(8,128)S(1)} %add.30), channel_id=1, source_target_pairs={{0,8},{4,12},{8,0},{12,4},{1,9},{5,13},{9,1},{13,5},{2,10},{6,14},... | collective-permute-start | bytes 307208 | tf_op jit(solution)/shard_map/ppermute | solution.py:336
  18.4 2.7 %collective-permute-done.3 = f32[200,128]{1,0:T(8,128)S(1)} collective-permute-done((f32[200,128]{1,0:T(8,128)S(1)}, f32[200,128]{1,0:T(8,128)S(1)}, u32[]{:S(2)}, u32[]{:S(2)}) %collective-permute-start.3) | collective-permute-done | bytes 102432 | tf_op jit(solution)/shard_map/ppermute | solution.py:336
  21.1 0.1 collective-permute-start.4
  21.2 1.2 %collective-permute-done.4.theirs_ref = f32[136,128]{1,0:T(8,128)S(1)} collective-permute-done((f32[136,128]{1,0:T(8,128)S(1)}, f32[136,128]{1,0:T(8,128)S(1)}, u32[]{:S(2)}, u32[]{:S(2)}) %collective-permute-start.4) | collective-permute-done | bytes 69664 | tf_op jit(solution)/shard_map/ppermute | solution.py:336
  22.4 0.0 copy-done
  22.4 7.6 %factor.1 = (f32[256,256]{1,0:T(8,128)}, bf16[3072,256]{1,0:T(8,128)(2,1)}, f32[32,64]{1,0:T(8,128)}) custom-call(f32[200,128]{1,0:T(8,128)S(1)} %add.31.mine_ref, f32[136,128]{1,0:T(8,128)S(1)} %collective-permute-done.4.theirs_ref, bf16[3072,256]{1,0:T(8,128)(2,1)S(1)} %copy-done), custom_call_target="tpu_custom_call" | custom-call | tf_op jit(solution)/shard_map/factor/pallas_call | solution.py:307
  (9 shorter events, 0.1 us)
Async XLA Ops:
  3.0 19.5 %copy-start = (bf16[3072,256]{1,0:T(8,128)(2,1)S(1)}, bf16[3072,256]{1,0:T(8,128)(2,1)}, u32[]{:S(2)}) copy-start(bf16[3072,256]{1,0:T(8,128)(2,1)} %sketch_hbm.3) | copy-start | bytes 4718596
  3.0 1.5 %collective-permute-start = (f32[264,128]{1,0:T(8,128)S(1)}, f32[264,128]{1,0:T(8,128)S(1)}, u32[]{:S(2)}, u32[]{:S(2)}) collective-permute-start(f32[264,128]{1,0:T(8,128)S(1)} %get-tuple-element.9), channel_id=1, source_target_pairs={{0,1},{1,0},{2,3},{3,2},{4,5},{5,4},{6,7},{7,6},{8,9},{9,8},{10,11... | collective-permute-start | bytes 405512 | tf_op jit(solution)/shard_map/ppermute | solution.py:336
  4.6 6.1 %collective-permute-start.1 = (f32[200,128]{1,0:T(8,128)S(1)}, f32[200,128]{1,0:T(8,128)S(1)}, u32[]{:S(2)}, u32[]{:S(2)}) collective-permute-start(f32[200,128]{1,0:T(8,128)S(1)} %pad_maximum_fusion), channel_id=1, source_target_pairs={{0,2},{1,3},{2,0},{3,1},{4,6},{5,7},{6,4},{7,5},{8,10},{9,11},{10,... | collective-permute-start | bytes 307208 | tf_op jit(solution)/shard_map/ppermute | solution.py:336
  10.7 4.7 %collective-permute-start.2 = (f32[200,128]{1,0:T(8,128)S(1)}, f32[200,128]{1,0:T(8,128)S(1)}, u32[]{:S(2)}, u32[]{:S(2)}) collective-permute-start(f32[200,128]{1,0:T(8,128)S(1)} %fusion), channel_id=1, source_target_pairs={{0,4},{4,0},{8,12},{12,8},{1,5},{5,1},{9,13},{13,9},{2,6},{6,2},{1... | collective-permute-start | bytes 307208 | tf_op jit(solution)/shard_map/ppermute | solution.py:336
  15.5 5.6 %collective-permute-start.3 = (f32[200,128]{1,0:T(8,128)S(1)}, f32[200,128]{1,0:T(8,128)S(1)}, u32[]{:S(2)}, u32[]{:S(2)}) collective-permute-start(f32[200,128]{1,0:T(8,128)S(1)} %add.30), channel_id=1, source_target_pairs={{0,8},{4,12},{8,0},{12,4},{1,9},{5,13},{9,1},{13,5},{2,10},{6,14},... | collective-permute-start | bytes 307208 | tf_op jit(solution)/shard_map/ppermute | solution.py:336
  21.1 1.3 %collective-permute-start.4 = (f32[136,128]{1,0:T(8,128)S(1)}, f32[136,128]{1,0:T(8,128)S(1)}, u32[]{:S(2)}, u32[]{:S(2)}) collective-permute-start(f32[136,128]{1,0:T(8,128)S(1)} %slice.14), channel_id=1, source_target_pairs={{0,1},{1,0},{2,3},{3,2},{4,5},{5,4},{6,7},{7,6},{8,9},{9,8},{10,11... | collective-permute-start | bytes 208904 | tf_op jit(solution)/shard_map/ppermute | solution.py:336

commit v5 on v4

--- a/solution.py
+++ b/solution.py
@@ -109,7 +109,7 @@
     return high, middle, low
 
 
-def eliminate(a_ref, one_ref, scale, unscale, r_ref, x_ref):
+def eliminate(a_ref, one_ref, r_ref, x_ref, meanwhile=None):
     k = a_ref.shape[0]
     halves, panels = k // LANES, k // SUB
     shape = (SUB, LANES)
@@ -133,9 +133,10 @@
     def column_of(v, i):
         return jnp.broadcast_to(v[:, i : i + 1], shape)
 
-    def follow(target, panel, pivots):
+    def follow(target, panel, pivots, coefs=None):
         half, first = divmod(panel * SUB, LANES)
-        coefs = [column_of(target[half], first + i) for i in range(SUB)]
+        if coefs is None:
+            coefs = [column_of(target[half], first + i) for i in range(SUB)]
         inside = (lane >= first) & (lane < first + SUB)
         rest = list(target)
         rest[half] = jnp.where(inside, 0.0, rest[half])
@@ -143,10 +144,13 @@
             rest[h] - tree_sum([coefs[i] * pivots[i][h] for i in range(SUB)]) for h in range(halves)
         ]
 
-    def solve(panel, block):
+    def columns(panel, block):
         half, first = divmod(panel * SUB, LANES)
-        block = list(block)
-        cols = [column_of(block[half], first + i) * one for i in range(SUB)]
+        return [column_of(block[half], first + i) * one for i in range(SUB)]
+
+    def solve(panel, block, cols, under=None, corner=None):
+        half, first = divmod(panel * SUB, LANES)
+        block, cols = list(block), list(cols)
         saved = [jnp.zeros(shape, jnp.float32)] * halves
         roots = jnp.zeros(shape, jnp.float32)
         for i in range(0, SUB, 2):
@@ -179,15 +183,30 @@
             )
             pair = (lane == first + i) | (lane == first + i + 1)
             block[half] = jnp.where(pair, unit, block[half])
+            if under is not None:
+                left, right = under[i], under[i + 1]
+                by_upper = left * r - right * q
+                by_lower = right * p - left * q
+
+                def step_under(v, upper_value, lower_value):
+                    return v - (upper_value * by_upper + lower_value * by_lower) * inverse
+
+                corner = [
+                    step_under(c, row_of(left, j), row_of(right, j)) for j, c in enumerate(corner)
+                ]
+                under = [
+                    step_under(u, row_of(cols[j], i), row_of(cols[j], i + 1)) if j > i + 1 else u
+                    for j, u in enumerate(under)
+                ]
             cols = [step(c) if j > i + 1 else c for j, c in enumerate(cols)]
             block = [step(v) for v in block]
         for h in range(halves):
             ahead = lane + h * LANES - (sub + panel * SUB)
             z = saved[h] * roots
             inverse_part = jnp.where(ahead < 0, z, jnp.where(ahead == 0, roots, 0.0))
-            r_ref[rows_of(panel), lanes_of(h)] = jnp.where(ahead >= 0, z, 0.0) * unscale[h]
-            x_ref[rows_of(panel), lanes_of(h)] = inverse_part * scale[h]
-        return block
+            r_ref[rows_of(panel), lanes_of(h)] = jnp.where(ahead >= 0, z, 0.0)
+            x_ref[rows_of(panel), lanes_of(h)] = inverse_part
+        return block, corner
 
     per = 4
     size = per * SUB
@@ -199,17 +218,27 @@
         befores, afters = [], []
         for panel in range(number * per, (number + 1) * per):
             before = load(panel) if ahead_block is None else ahead_block
-            after = solve(panel, before)
+            if panel % 2 == 0:
+                lower = load(panel + 1)
+                under = columns(panel, lower)
+                after, corner = solve(
+                    panel, before, columns(panel, before), under, columns(panel + 1, lower)
+                )
+            else:
+                under = None
+                after, _ = solve(panel, before, corner)
             befores.append(jnp.concatenate(before, 1))
             afters.append(jnp.concatenate(after, 1))
             pivots = [[row_of(v, i) for v in after] for i in range(SUB)]
             for other in range(panel + 1, min((number + 2) * per, panels)):
-                target = follow(load(other), panel, pivots)
+                target = follow(load(other), panel, pivots, under if other == panel + 1 else None)
                 if other == panel + 1:
                     ahead_block = target
                     continue
                 for h in range(halves):
                     a_ref[rows_of(other), lanes_of(h)] = target[h]
+            if meanwhile is not None:
+                meanwhile(panel)
         if number + 2 >= blocks:
             continue
         low = number * size
@@ -229,49 +258,147 @@
         a_ref[top:k, :] = jnp.where(inside, 0.0, a_ref[top:k, :]) - change
 
 
-def factor_kernel(
-    steps, cells, mine_ref, theirs_ref, sketch_hbm, r_hbm, basis_hbm, proj_hbm,
-    a_ref, one_ref, r_ref, x_ref, proj_ref, sketch, basis, sem_in, sem_r, sem_proj, sems,
+def exact_dot(left, right, over):
+    return lax.dot_general(
+        left,
+        right,
+        (((1,), (over,)), ((), ())),
+        precision=HIGHEST,
+        preferred_element_type=jnp.float32,
+    )
+
+
+def scales_of(tile_ref, n):
+    norms = [tile_ref[n + i : n + i + 1, :] for i in range(2)]
+    scale = [lax.rsqrt(v) for v in norms]
+    across = [jnp.broadcast_to(s, (n, n)) for s in scale]
+    return scale, [v * s for v, s in zip(norms, scale)], across, [s.T for s in across]
+
+
+def top_kernel(both_ref, out_ref, a_ref, one_ref, r_ref, x_ref):
+    n = both_ref.shape[1]
+    second = lax.axis_index("grp") % 2 == 1
+
+    @pl.when(jnp.logical_not(second))
+    def _():
+        out_ref[0:n, :] = both_ref[0:n, :]
+        out_ref[n : 2 * n, :] = jnp.zeros((n, n), jnp.float32)
+
+    @pl.when(second)
+    def _():
+        one_ref[...] = jnp.ones_like(one_ref)
+        row = lax.broadcasted_iota(jnp.int32, (n, n), 0)
+        col = lax.broadcasted_iota(jnp.int32, (n, n), 1)
+        scale = lax.rsqrt(both_ref[n : n + 1, :])
+        across = jnp.broadcast_to(scale, (n, n))
+        packed = both_ref[0:n, :]
+        whole = jnp.where(row > col, packed, packed.T) * across * across.T
+        a_ref[...] = jnp.where(row == col, 1.0, whole)
+        eliminate(a_ref, one_ref, r_ref, x_ref)
+        out_ref[0:n, :] = jnp.where(row >= col, x_ref[...], r_ref[...])
+        out_ref[n : 2 * n, :] = packed
+
+
+def factor_top(both):
+    n = both.shape[1]
+    vmem = pl.BlockSpec(memory_space=pltpu.VMEM)
+    return pl.pallas_call(
+        top_kernel,
+        out_shape=jax.ShapeDtypeStruct((2 * n, n), jnp.float32),
+        in_specs=[vmem],
+        out_specs=vmem,
+        scratch_shapes=[
+            pltpu.VMEM((n, n), jnp.float32),
+            pltpu.VMEM((SUB, LANES), jnp.float32),
+            pltpu.VMEM((n, n), jnp.float32),
+            pltpu.VMEM((n, n), jnp.float32),
+        ],
+        compiler_params=pltpu.CompilerParams(vmem_limit_bytes=VMEM_LIMIT),
+        name="factor_top",
+    )(both)
+
+
+def rest_kernel(
+    steps, early, cells, own_ref, theirs_ref, both_ref, sketch_hbm, r_hbm, basis_hbm, proj_hbm,
+    a_ref, one_ref, low_r_ref, low_x_ref, r_ref, x_ref, proj_ref, sketch, basis,
+    sem_in, sem_r, sem_proj, sems, early_sems,
 ):
     copy_in = pltpu.make_async_copy(sketch_hbm, sketch, sem_in)
     copy_in.start()
-    k = a_ref.shape[0]
+    k = r_ref.shape[0]
     n = k // 2
     one_ref[...] = jnp.ones_like(one_ref)
     first = lax.axis_index("grp") % 2 == 0
-    square = jnp.where(first, mine_ref[0:n, :], theirs_ref[0:n, :])
-    packed = jnp.where(first, theirs_ref[0:n, :], mine_ref[0:n, :])
     row = lax.broadcasted_iota(jnp.int32, (n, n), 0)
     col = lax.broadcasted_iota(jnp.int32, (n, n), 1)
-    norms = [mine_ref[n + i : n + i + 1, :] for i in range(2)]
-    scale = [lax.rsqrt(v) for v in norms]
-    unscale = [v * s for v, s in zip(norms, scale)]
-    across = [jnp.broadcast_to(s, (n, n)) for s in scale]
-    down = [s.T for s in across]
-    turned = packed.T
-    a_ref[0:n, 0:n] = jnp.where(row >= col, packed, turned) * across[0] * down[0]
-    below = jnp.where(row < col, packed, turned) * across[1] * down[1]
-    a_ref[n:k, n:k] = jnp.where(row == col, 1.0, below)
-    a_ref[0:n, n:k] = square.T * across[1] * down[0]
-    a_ref[n:k, 0:n] = square * across[0] * down[1]
-    eliminate(a_ref, one_ref, scale, unscale, r_ref, x_ref)
+    zero = jnp.zeros((n, n), jnp.float32)
+    square = jnp.where(first, own_ref[0:n, :], theirs_ref[0:n, :])
+    done = jnp.where(first, theirs_ref[0:n, :], own_ref[0:n, :])
+    packed = jnp.where(first, theirs_ref[n:k, :], own_ref[n:k, :])
+    scale, unscale, across, down = scales_of(both_ref, n)
+    top_x = jnp.where(row >= col, done, zero)
+    low_top = exact_dot(square * across[0] * down[1], top_x, 1)
+    low_low = jnp.where(row < col, packed, packed.T) * across[1] * down[1]
+    a_ref[...] = jnp.where(row == col, 1.0, low_low) - exact_dot(low_top, low_top, 1)
+    r_ref[0:n, 0:n] = jnp.where(row < col, done, jnp.where(row == col, 1.0 / done, zero)) * unscale[0]
+    r_ref[0:n, n:k] = low_top.T * unscale[1]
+    r_ref[n:k, 0:n] = zero
+    top_x_out = top_x * scale[0]
+    x_ref[0:n, 0:n] = top_x_out
+    x_ref[0:n, n:k] = zero
+    back = exact_dot(low_top, top_x_out, 0)
+    contract = (((1,), (1,)), ((), ()))
+    high, middle, low = split3(top_x_out)
+    top_parts = jnp.concatenate(
+        [jnp.concatenate([high, middle], 1), jnp.concatenate([low, jnp.zeros_like(low)], 1)], 0
+    )
+    total_rows = sketch.shape[0]
+    size = total_rows // early
+    copies = []
+
+    def first_columns(panel):
+        if panel == 1:
+            copy_in.wait()
+        index = panel - 2
+        if not 0 <= index < early:
+            return
+        rows = pl.ds(index * size, size)
+        piece = sketch[rows, 0:n]
+        pair = lax.dot_general(
+            jnp.concatenate([piece, piece], 1),
+            top_parts,
+            contract,
+            preferred_element_type=jnp.float32,
+        )
+        basis[rows, 0:n] = (pair[:, n:k] + pair[:, 0:n]).astype(basis.dtype)
+        at = pl.ds(0, n)
+        copy = pltpu.make_async_copy(
+            basis.at[rows, at], basis_hbm.at[rows, at], early_sems.at[index]
+        )
+        copy.start()
+        copies.append(copy)
+
+    eliminate(a_ref, one_ref, low_r_ref, low_x_ref, first_columns)
+    r_ref[n:k, n:k] = low_r_ref[...] * unscale[1]
     copy_r = pltpu.make_async_copy(r_ref, r_hbm, sem_r)
     copy_r.start()
-    copies = [copy_r]
-    parts = split3(x_ref[...])
-    copy_in.wait()
-    size = sketch.shape[0] // steps
+    copies.append(copy_r)
+    low_x = low_x_ref[...]
+    low_left = -exact_dot(low_x, back, 0)
+    low_right = low_x * scale[1]
+    x_ref[n:k, 0:n] = low_left
+    x_ref[n:k, n:k] = low_right
+    high, middle, low = split3(jnp.concatenate([low_left, low_right], 1))
+    paired = jnp.concatenate([high, middle], 0)
+    size = total_rows // steps
     for step in range(steps):
         rows = pl.ds(step * size, size)
         piece = sketch[rows, :]
-        total = None
-        for part in parts[::-1]:
-            term = lax.dot_general(
-                piece, part, (((1,), (1,)), ((), ())), preferred_element_type=jnp.float32
-            )
-            total = term if total is None else total + term
-        basis[rows, :] = total.astype(basis.dtype)
-        copy = pltpu.make_async_copy(basis.at[rows], basis_hbm.at[rows], sems.at[step])
+        pair = lax.dot_general(piece, paired, contract, preferred_element_type=jnp.float32)
+        total = lax.dot_general(piece, low, contract, preferred_element_type=jnp.float32)
+        basis[rows, n:k] = (total + pair[:, n:k] + pair[:, 0:n]).astype(basis.dtype)
+        at = pl.ds(n, n)
+        copy = pltpu.make_async_copy(basis.at[rows, at], basis_hbm.at[rows, at], sems.at[step])
         copy.start()
         copies.append(copy)
         if step:
@@ -282,12 +409,8 @@
         total = None
         for h in range(k // LANES):
             at = n + SUB + h * days
-            term = lax.dot_general(
-                mine_ref[at : at + days, :],
-                x_ref[own_rows, h * LANES : (h + 1) * LANES],
-                (((1,), (1,)), ((), ())),
-                precision=HIGHEST,
-                preferred_element_type=jnp.float32,
+            term = exact_dot(
+                both_ref[at : at + days, :], x_ref[own_rows, h * LANES : (h + 1) * LANES], 1
             )
             total = term if total is None else total + term
         proj_ref[...] = total
@@ -298,24 +421,28 @@
         copy.wait()
 
 
-def factor(mine, theirs, sketch, cells):
+def factor_rest(own, theirs, both, sketch, cells):
     rows, k = sketch.shape
-    days = (mine.shape[0] - theirs.shape[0]) * LANES // k
+    n = k // 2
+    days = (both.shape[0] - n - SUB) * LANES // k
     steps = chunks_of(rows, 6)
+    early = chunks_of(rows, n // SUB - 4)
     hbm = pl.BlockSpec(memory_space=pltpu.HBM)
     vmem = pl.BlockSpec(memory_space=pltpu.VMEM)
     return pl.pallas_call(
-        functools.partial(factor_kernel, steps, cells),
+        functools.partial(rest_kernel, steps, early, cells),
         out_shape=(
             jax.ShapeDtypeStruct((k, k), jnp.float32),
             jax.ShapeDtypeStruct((rows, k), jnp.bfloat16),
             jax.ShapeDtypeStruct((days, k // cells), jnp.float32),
         ),
-        in_specs=[vmem, vmem, hbm],
+        in_specs=[vmem, vmem, vmem, hbm],
         out_specs=(hbm, hbm, hbm),
         scratch_shapes=[
-            pltpu.VMEM((k, k), jnp.float32),
+            pltpu.VMEM((n, n), jnp.float32),
             pltpu.VMEM((SUB, LANES), jnp.float32),
+            pltpu.VMEM((n, n), jnp.float32),
+            pltpu.VMEM((n, n), jnp.float32),
             pltpu.VMEM((k, k), jnp.float32),
             pltpu.VMEM((k, k), jnp.float32),
             pltpu.VMEM((days, k // cells), jnp.float32),
@@ -325,10 +452,11 @@
             pltpu.SemaphoreType.DMA,
             pltpu.SemaphoreType.DMA,
             pltpu.SemaphoreType.DMA((steps,)),
+            pltpu.SemaphoreType.DMA((early,)),
         ],
         compiler_params=pltpu.CompilerParams(vmem_limit_bytes=VMEM_LIMIT),
-        name="factor",
-    )(mine, theirs, sketch)
+        name="factor_rest",
+    )(own, theirs, both, sketch)
 
 
 def swap(value, axis, bit):
@@ -356,8 +484,9 @@
     while bit < cells:
         both = both + swap(both, "cell", bit)
         bit *= 2
-    theirs = swap(both[:shared], "grp", 1)
-    r_factor, basis, projected = factor(both, theirs, sketch, cells)
+    own = factor_top(both)
+    theirs = swap(own, "grp", 1)
+    r_factor, basis, projected = factor_rest(own, theirs, both, sketch, cells)
     return r_factor, basis, projected.T
 
 

time: 30.3 us -> 28.5 us (0.941)
  Pallas kernels: 9.91 us -> 7.78 us
  starting transfers between devices: 8.29 us -> 9.05 us
    pallas_call x1 -> x2, Pallas kernels: 7.56 us -> 5.44 us  [the longest x1 5.41 us: factor_rest(): pl.pallas_call(functools.partial(rest_kernel, steps, early, cells), out_s...]
    ppermute x5, starting transfers between devices: 8.29 us -> 9.05 us  [swap(): return lax.ppermute(value, axis, [(i, i ^ bit) for i in range(size)])]
where the time goes in v5:
time: 28.5 us; the launch traced here: 28.4 us
  waiting for transfers between devices  10.7 us (38%)
  starting transfers between devices  9.05 us (32%)
  Pallas kernels  7.78 us (27%)
  between operations  0.7 us (2%)
    ppermute x5, waiting for transfers between devices, swap(): return lax.ppermute(value, axis, [(i, i ^ bit) for i in range(size)])  10.7 us
    ppermute x5, starting transfers between devices, swap(): return lax.ppermute(value, axis, [(i, i ^ bit) for i in range(size)])  9.05 us
    pallas_call x1, Pallas kernels, factor_rest(): pl.pallas_call(functools.partial(rest_kernel, steps, early, cells), out_s...  5.41 us
    pallas_call x1, Pallas kernels, local_stats(): pl.pallas_call(functools.partial(stats_kernel, steps, groups), out_shape=...  2.35 us
  transfers between devices with their start and end apart: 5, of which 5 were waited for; matrix products, arithmetic and copies ran while one was open for 0% of the time, Pallas kernels for 0%

profile of v5, /device:TPU:0, one launch (start us, length us, event | category | flops | bytes accessed | tf_op | source)
XLA Modules:
  0.0 28.4 jit_solution(14704119706977321409)
XLA Ops:
  0.6 2.3 %local_stats.1 = (f32[264,128]{1,0:T(8,128)S(1)}, f32[264,128]{1,0:T(8,128)S(1)}) custom-call(bf16[3072,256]{1,0:T(8,128)(2,1)} %sketch_hbm.3, bf16[3072,128]{1,0:T(8,128)(2,1)} %slab_hbm.1), custom_call_target="tpu_custom_call" | custom-call | tf_op jit(solution)/shard_map/local_stats/pallas_call | solution.py:80
  3.0 0.0 copy-start
  3.0 0.5 %collective-permute-start = (f32[264,128]{1,0:T(8,128)S(1)}, f32[264,128]{1,0:T(8,128)S(1)}, u32[]{:S(2)}, u32[]{:S(2)}) collective-permute-start(f32[264,128]{1,0:T(8,128)S(1)} %get-tuple-element.9), channel_id=1, source_target_pairs={{0,1},{1,0},{2,3},{3,2},{4,5},{5,4},{6,7},{7,6},{8,9},{9,8},{10,11... | collective-permute-start | bytes 405512 | tf_op jit(solution)/shard_map/ppermute | solution.py:464
  3.5 1.0 %collective-permute-done = f32[264,128]{1,0:T(8,128)S(1)} collective-permute-done((f32[264,128]{1,0:T(8,128)S(1)}, f32[264,128]{1,0:T(8,128)S(1)}, u32[]{:S(2)}, u32[]{:S(2)}) %collective-permute-start) | collective-permute-done | bytes 135200 | tf_op jit(solution)/shard_map/ppermute | solution.py:464
  4.6 2.9 %collective-permute-start.1 = (f32[200,128]{1,0:T(8,128)S(1)}, f32[200,128]{1,0:T(8,128)S(1)}, u32[]{:S(2)}, u32[]{:S(2)}) collective-permute-start(f32[200,128]{1,0:T(8,128)S(1)} %pad_maximum_fusion), channel_id=1, source_target_pairs={{0,2},{1,3},{2,0},{3,1},{4,6},{5,7},{6,4},{7,5},{8,10},{9,11},{10,... | collective-permute-start | bytes 307208 | tf_op jit(solution)/shard_map/ppermute | solution.py:464
  7.5 3.2 %collective-permute-done.1 = f32[200,128]{1,0:T(8,128)S(1)} collective-permute-done((f32[200,128]{1,0:T(8,128)S(1)}, f32[200,128]{1,0:T(8,128)S(1)}, u32[]{:S(2)}, u32[]{:S(2)}) %collective-permute-start.1) | collective-permute-done | bytes 102432 | tf_op jit(solution)/shard_map/ppermute | solution.py:464
  10.7 1.9 %collective-permute-start.2 = (f32[200,128]{1,0:T(8,128)S(1)}, f32[200,128]{1,0:T(8,128)S(1)}, u32[]{:S(2)}, u32[]{:S(2)}) collective-permute-start(f32[200,128]{1,0:T(8,128)S(1)} %fusion), channel_id=1, source_target_pairs={{0,4},{4,0},{8,12},{12,8},{1,5},{5,1},{9,13},{13,9},{2,6},{6,2},{1... | collective-permute-start | bytes 307208 | tf_op jit(solution)/shard_map/ppermute | solution.py:464
  12.6 2.8 %collective-permute-done.2 = f32[200,128]{1,0:T(8,128)S(1)} collective-permute-done((f32[200,128]{1,0:T(8,128)S(1)}, f32[200,128]{1,0:T(8,128)S(1)}, u32[]{:S(2)}, u32[]{:S(2)}) %collective-permute-start.2) | collective-permute-done | bytes 102432 | tf_op jit(solution)/shard_map/ppermute | solution.py:464
  15.5 2.9 %collective-permute-start.3 = (f32[200,128]{1,0:T(8,128)S(1)}, f32[200,128]{1,0:T(8,128)S(1)}, u32[]{:S(2)}, u32[]{:S(2)}) collective-permute-start(f32[200,128]{1,0:T(8,128)S(1)} %add.30), channel_id=1, source_target_pairs={{0,8},{4,12},{8,0},{12,4},{1,9},{5,13},{9,1},{13,5},{2,10},{6,14},... | collective-permute-start | bytes 307208 | tf_op jit(solution)/shard_map/ppermute | solution.py:464
  18.4 2.7 %collective-permute-done.3 = f32[200,128]{1,0:T(8,128)S(1)} collective-permute-done((f32[200,128]{1,0:T(8,128)S(1)}, f32[200,128]{1,0:T(8,128)S(1)}, u32[]{:S(2)}, u32[]{:S(2)}) %collective-permute-start.3) | collective-permute-done | bytes 102432 | tf_op jit(solution)/shard_map/ppermute | solution.py:464
  21.1 0.8 %collective-permute-start.4 = (f32[256,128]{1,0:T(8,128)S(1)}, f32[256,128]{1,0:T(8,128)S(1)}, u32[]{:S(2)}, u32[]{:S(2)}) collective-permute-start(f32[256,128]{1,0:T(8,128)S(1)} %factor_top.1.own_ref), channel_id=1, source_target_pairs={{0,1},{1,0},{2,3},{3,2},{4,5},{5,4},{6,7},{7,6},{8,9},{9,8},{10,11... | collective-permute-start | bytes 393224 | tf_op jit(solution)/shard_map/ppermute | solution.py:464
  22.0 1.0 %collective-permute-done.4.theirs_ref = f32[256,128]{1,0:T(8,128)S(1)} collective-permute-done((f32[256,128]{1,0:T(8,128)S(1)}, f32[256,128]{1,0:T(8,128)S(1)}, u32[]{:S(2)}, u32[]{:S(2)}) %collective-permute-start.4) | collective-permute-done | bytes 131104 | tf_op jit(solution)/shard_map/ppermute | solution.py:464
  23.0 0.0 copy-done
  23.0 5.4 %factor_rest.1 = (f32[256,256]{1,0:T(8,128)}, bf16[3072,256]{1,0:T(8,128)(2,1)}, f32[32,64]{1,0:T(8,128)}) custom-call(f32[256,128]{1,0:T(8,128)S(1)} %factor_top.1.own_ref, f32[256,128]{1,0:T(8,128)S(1)} %collective-permute-done.4.theirs_ref, f32[200,128]{1,0:T(8,128)S(1)} %add.31.both_ref, bf16[3072,256]{1,0:T(8,128)(2,1)S(1)} %copy-done), custom_call_target="tpu_custom_call" | custom-call | tf_op jit(solution)/shard_map/factor_rest/pallas_call | solution.py:432
  (9 shorter events, 0.1 us)
Async XLA Ops:
  3.0 20.0 %copy-start = (bf16[3072,256]{1,0:T(8,128)(2,1)S(1)}, bf16[3072,256]{1,0:T(8,128)(2,1)}, u32[]{:S(2)}) copy-start(bf16[3072,256]{1,0:T(8,128)(2,1)} %sketch_hbm.3) | copy-start | bytes 4718596
  3.0 1.5 %collective-permute-start = (f32[264,128]{1,0:T(8,128)S(1)}, f32[264,128]{1,0:T(8,128)S(1)}, u32[]{:S(2)}, u32[]{:S(2)}) collective-permute-start(f32[264,128]{1,0:T(8,128)S(1)} %get-tuple-element.9), channel_id=1, source_target_pairs={{0,1},{1,0},{2,3},{3,2},{4,5},{5,4},{6,7},{7,6},{8,9},{9,8},{10,11... | collective-permute-start | bytes 405512 | tf_op jit(solution)/shard_map/ppermute | solution.py:464
  4.6 6.1 %collective-permute-start.1 = (f32[200,128]{1,0:T(8,128)S(1)}, f32[200,128]{1,0:T(8,128)S(1)}, u32[]{:S(2)}, u32[]{:S(2)}) collective-permute-start(f32[200,128]{1,0:T(8,128)S(1)} %pad_maximum_fusion), channel_id=1, source_target_pairs={{0,2},{1,3},{2,0},{3,1},{4,6},{5,7},{6,4},{7,5},{8,10},{9,11},{10,... | collective-permute-start | bytes 307208 | tf_op jit(solution)/shard_map/ppermute | solution.py:464
  10.7 4.7 %collective-permute-start.2 = (f32[200,128]{1,0:T(8,128)S(1)}, f32[200,128]{1,0:T(8,128)S(1)}, u32[]{:S(2)}, u32[]{:S(2)}) collective-permute-start(f32[200,128]{1,0:T(8,128)S(1)} %fusion), channel_id=1, source_target_pairs={{0,4},{4,0},{8,12},{12,8},{1,5},{5,1},{9,13},{13,9},{2,6},{6,2},{1... | collective-permute-start | bytes 307208 | tf_op jit(solution)/shard_map/ppermute | solution.py:464
  15.5 5.6 %collective-permute-start.3 = (f32[200,128]{1,0:T(8,128)S(1)}, f32[200,128]{1,0:T(8,128)S(1)}, u32[]{:S(2)}, u32[]{:S(2)}) collective-permute-start(f32[200,128]{1,0:T(8,128)S(1)} %add.30), channel_id=1, source_target_pairs={{0,8},{4,12},{8,0},{12,4},{1,9},{5,13},{9,1},{13,5},{2,10},{6,14},... | collective-permute-start | bytes 307208 | tf_op jit(solution)/shard_map/ppermute | solution.py:464
  21.1 1.8 %collective-permute-start.4 = (f32[256,128]{1,0:T(8,128)S(1)}, f32[256,128]{1,0:T(8,128)S(1)}, u32[]{:S(2)}, u32[]{:S(2)}) collective-permute-start(f32[256,128]{1,0:T(8,128)S(1)} %factor_top.1.own_ref), channel_id=1, source_target_pairs={{0,1},{1,0},{2,3},{3,2},{4,5},{5,4},{6,7},{7,6},{8,9},{9,8},{10,11... | collective-permute-start | bytes 393224 | tf_op jit(solution)/shard_map/ppermute | solution.py:464

commit v6 on v5

--- a/solution.py
+++ b/solution.py
@@ -259,13 +259,19 @@
 
 
 def exact_dot(left, right, over):
-    return lax.dot_general(
-        left,
-        right,
-        (((1,), (over,)), ((), ())),
-        precision=HIGHEST,
-        preferred_element_type=jnp.float32,
-    )
+    left_high, left_middle, left_low = split3(left)
+    high, middle, low = split3(right)
+
+    def two(first, second, by_first, by_second):
+        return lax.dot_general(
+            jnp.concatenate([first, second], 1),
+            jnp.concatenate([by_first, by_second], over),
+            (((1,), (over,)), ((), ())),
+            preferred_element_type=jnp.float32,
+        )
+
+    small = two(left_middle, left_low, middle, high) + two(left_high, left_high, low, middle)
+    return small + two(left_middle, left_high, high, high)
 
 
 def scales_of(tile_ref, n):

time: 28.5 us -> 28.1 us (0.986)
  Pallas kernels: 7.78 us -> 7.39 us
    pallas_call x1, Pallas kernels: 5.41 us -> 5.01 us  [factor_rest(): pl.pallas_call(functools.partial(rest_kernel, steps, early, cells), out_s...]
where the time goes in v6:
time: 28.1 us; the launch traced here: 28 us
  waiting for transfers between devices  10.7 us (38%)
  starting transfers between devices  9.05 us (32%)
  Pallas kernels  7.39 us (26%)
  between operations  0.7 us (2%)
    ppermute x5, waiting for transfers between devices, swap(): return lax.ppermute(value, axis, [(i, i ^ bit) for i in range(size)])  10.7 us
    ppermute x5, starting transfers between devices, swap(): return lax.ppermute(value, axis, [(i, i ^ bit) for i in range(size)])  9.05 us
    pallas_call x1, Pallas kernels, factor_rest(): pl.pallas_call(functools.partial(rest_kernel, steps, early, cells), out_s...  5.01 us
    pallas_call x1, Pallas kernels, local_stats(): pl.pallas_call(functools.partial(stats_kernel, steps, groups), out_shape=...  2.35 us
  transfers between devices with their start and end apart: 5, of which 5 were waited for; matrix products, arithmetic and copies ran while one was open for 0% of the time, Pallas kernels for 0%

profile of v6, /device:TPU:0, one launch (start us, length us, event | category | flops | bytes accessed | tf_op | source)
XLA Modules:
  0.0 28.0 jit_solution(8730402025941337534)
XLA Ops:
  0.6 2.3 %local_stats.1 = (f32[264,128]{1,0:T(8,128)S(1)}, f32[264,128]{1,0:T(8,128)S(1)}) custom-call(bf16[3072,256]{1,0:T(8,128)(2,1)} %sketch_hbm.3, bf16[3072,128]{1,0:T(8,128)(2,1)} %slab_hbm.1), custom_call_target="tpu_custom_call" | custom-call | tf_op jit(solution)/shard_map/local_stats/pallas_call | solution.py:80
  3.0 0.0 copy-start
  3.0 0.5 %collective-permute-start = (f32[264,128]{1,0:T(8,128)S(1)}, f32[264,128]{1,0:T(8,128)S(1)}, u32[]{:S(2)}, u32[]{:S(2)}) collective-permute-start(f32[264,128]{1,0:T(8,128)S(1)} %get-tuple-element.9), channel_id=1, source_target_pairs={{0,1},{1,0},{2,3},{3,2},{4,5},{5,4},{6,7},{7,6},{8,9},{9,8},{10,11... | collective-permute-start | bytes 405512 | tf_op jit(solution)/shard_map/ppermute | solution.py:470
  3.5 1.0 %collective-permute-done = f32[264,128]{1,0:T(8,128)S(1)} collective-permute-done((f32[264,128]{1,0:T(8,128)S(1)}, f32[264,128]{1,0:T(8,128)S(1)}, u32[]{:S(2)}, u32[]{:S(2)}) %collective-permute-start) | collective-permute-done | bytes 135200 | tf_op jit(solution)/shard_map/ppermute | solution.py:470
  4.6 2.9 %collective-permute-start.1 = (f32[200,128]{1,0:T(8,128)S(1)}, f32[200,128]{1,0:T(8,128)S(1)}, u32[]{:S(2)}, u32[]{:S(2)}) collective-permute-start(f32[200,128]{1,0:T(8,128)S(1)} %pad_maximum_fusion), channel_id=1, source_target_pairs={{0,2},{1,3},{2,0},{3,1},{4,6},{5,7},{6,4},{7,5},{8,10},{9,11},{10,... | collective-permute-start | bytes 307208 | tf_op jit(solution)/shard_map/ppermute | solution.py:470
  7.5 3.2 %collective-permute-done.1 = f32[200,128]{1,0:T(8,128)S(1)} collective-permute-done((f32[200,128]{1,0:T(8,128)S(1)}, f32[200,128]{1,0:T(8,128)S(1)}, u32[]{:S(2)}, u32[]{:S(2)}) %collective-permute-start.1) | collective-permute-done | bytes 102432 | tf_op jit(solution)/shard_map/ppermute | solution.py:470
  10.7 1.9 %collective-permute-start.2 = (f32[200,128]{1,0:T(8,128)S(1)}, f32[200,128]{1,0:T(8,128)S(1)}, u32[]{:S(2)}, u32[]{:S(2)}) collective-permute-start(f32[200,128]{1,0:T(8,128)S(1)} %fusion), channel_id=1, source_target_pairs={{0,4},{4,0},{8,12},{12,8},{1,5},{5,1},{9,13},{13,9},{2,6},{6,2},{1... | collective-permute-start | bytes 307208 | tf_op jit(solution)/shard_map/ppermute | solution.py:470
  12.6 2.8 %collective-permute-done.2 = f32[200,128]{1,0:T(8,128)S(1)} collective-permute-done((f32[200,128]{1,0:T(8,128)S(1)}, f32[200,128]{1,0:T(8,128)S(1)}, u32[]{:S(2)}, u32[]{:S(2)}) %collective-permute-start.2) | collective-permute-done | bytes 102432 | tf_op jit(solution)/shard_map/ppermute | solution.py:470
  15.5 2.9 %collective-permute-start.3 = (f32[200,128]{1,0:T(8,128)S(1)}, f32[200,128]{1,0:T(8,128)S(1)}, u32[]{:S(2)}, u32[]{:S(2)}) collective-permute-start(f32[200,128]{1,0:T(8,128)S(1)} %add.30), channel_id=1, source_target_pairs={{0,8},{4,12},{8,0},{12,4},{1,9},{5,13},{9,1},{13,5},{2,10},{6,14},... | collective-permute-start | bytes 307208 | tf_op jit(solution)/shard_map/ppermute | solution.py:470
  18.4 2.7 %collective-permute-done.3 = f32[200,128]{1,0:T(8,128)S(1)} collective-permute-done((f32[200,128]{1,0:T(8,128)S(1)}, f32[200,128]{1,0:T(8,128)S(1)}, u32[]{:S(2)}, u32[]{:S(2)}) %collective-permute-start.3) | collective-permute-done | bytes 102432 | tf_op jit(solution)/shard_map/ppermute | solution.py:470
  21.1 0.8 %collective-permute-start.4 = (f32[256,128]{1,0:T(8,128)S(1)}, f32[256,128]{1,0:T(8,128)S(1)}, u32[]{:S(2)}, u32[]{:S(2)}) collective-permute-start(f32[256,128]{1,0:T(8,128)S(1)} %factor_top.1.own_ref), channel_id=1, source_target_pairs={{0,1},{1,0},{2,3},{3,2},{4,5},{5,4},{6,7},{7,6},{8,9},{9,8},{10,11... | collective-permute-start | bytes 393224 | tf_op jit(solution)/shard_map/ppermute | solution.py:470
  22.0 1.0 %collective-permute-done.4.theirs_ref = f32[256,128]{1,0:T(8,128)S(1)} collective-permute-done((f32[256,128]{1,0:T(8,128)S(1)}, f32[256,128]{1,0:T(8,128)S(1)}, u32[]{:S(2)}, u32[]{:S(2)}) %collective-permute-start.4) | collective-permute-done | bytes 131104 | tf_op jit(solution)/shard_map/ppermute | solution.py:470
  23.0 0.0 copy-done
  23.0 5.0 %factor_rest.1 = (f32[256,256]{1,0:T(8,128)}, bf16[3072,256]{1,0:T(8,128)(2,1)}, f32[32,64]{1,0:T(8,128)}) custom-call(f32[256,128]{1,0:T(8,128)S(1)} %factor_top.1.own_ref, f32[256,128]{1,0:T(8,128)S(1)} %collective-permute-done.4.theirs_ref, f32[200,128]{1,0:T(8,128)S(1)} %add.31.both_ref, bf16[3072,256]{1,0:T(8,128)(2,1)S(1)} %copy-done), custom_call_target="tpu_custom_call" | custom-call | tf_op jit(solution)/shard_map/factor_rest/pallas_call | solution.py:438
  (9 shorter events, 0.1 us)
Async XLA Ops:
  3.0 20.0 %copy-start = (bf16[3072,256]{1,0:T(8,128)(2,1)S(1)}, bf16[3072,256]{1,0:T(8,128)(2,1)}, u32[]{:S(2)}) copy-start(bf16[3072,256]{1,0:T(8,128)(2,1)} %sketch_hbm.3) | copy-start | bytes 4718596
  3.0 1.5 %collective-permute-start = (f32[264,128]{1,0:T(8,128)S(1)}, f32[264,128]{1,0:T(8,128)S(1)}, u32[]{:S(2)}, u32[]{:S(2)}) collective-permute-start(f32[264,128]{1,0:T(8,128)S(1)} %get-tuple-element.9), channel_id=1, source_target_pairs={{0,1},{1,0},{2,3},{3,2},{4,5},{5,4},{6,7},{7,6},{8,9},{9,8},{10,11... | collective-permute-start | bytes 405512 | tf_op jit(solution)/shard_map/ppermute | solution.py:470
  4.6 6.1 %collective-permute-start.1 = (f32[200,128]{1,0:T(8,128)S(1)}, f32[200,128]{1,0:T(8,128)S(1)}, u32[]{:S(2)}, u32[]{:S(2)}) collective-permute-start(f32[200,128]{1,0:T(8,128)S(1)} %pad_maximum_fusion), channel_id=1, source_target_pairs={{0,2},{1,3},{2,0},{3,1},{4,6},{5,7},{6,4},{7,5},{8,10},{9,11},{10,... | collective-permute-start | bytes 307208 | tf_op jit(solution)/shard_map/ppermute | solution.py:470
  10.7 4.7 %collective-permute-start.2 = (f32[200,128]{1,0:T(8,128)S(1)}, f32[200,128]{1,0:T(8,128)S(1)}, u32[]{:S(2)}, u32[]{:S(2)}) collective-permute-start(f32[200,128]{1,0:T(8,128)S(1)} %fusion), channel_id=1, source_target_pairs={{0,4},{4,0},{8,12},{12,8},{1,5},{5,1},{9,13},{13,9},{2,6},{6,2},{1... | collective-permute-start | bytes 307208 | tf_op jit(solution)/shard_map/ppermute | solution.py:470
  15.5 5.6 %collective-permute-start.3 = (f32[200,128]{1,0:T(8,128)S(1)}, f32[200,128]{1,0:T(8,128)S(1)}, u32[]{:S(2)}, u32[]{:S(2)}) collective-permute-start(f32[200,128]{1,0:T(8,128)S(1)} %add.30), channel_id=1, source_target_pairs={{0,8},{4,12},{8,0},{12,4},{1,9},{5,13},{9,1},{13,5},{2,10},{6,14},... | collective-permute-start | bytes 307208 | tf_op jit(solution)/shard_map/ppermute | solution.py:470
  21.1 1.8 %collective-permute-start.4 = (f32[256,128]{1,0:T(8,128)S(1)}, f32[256,128]{1,0:T(8,128)S(1)}, u32[]{:S(2)}, u32[]{:S(2)}) collective-permute-start(f32[256,128]{1,0:T(8,128)S(1)} %factor_top.1.own_ref), channel_id=1, source_target_pairs={{0,1},{1,0},{2,3},{3,2},{4,5},{5,4},{6,7},{7,6},{8,9},{9,8},{10,11... | collective-permute-start | bytes 393224 | tf_op jit(solution)/shard_map/ppermute | solution.py:470

commit v7 on v6

--- a/solution.py
+++ b/solution.py
@@ -325,12 +325,10 @@
 
 
 def rest_kernel(
-    steps, early, cells, own_ref, theirs_ref, both_ref, sketch_hbm, r_hbm, basis_hbm, proj_hbm,
-    a_ref, one_ref, low_r_ref, low_x_ref, r_ref, x_ref, proj_ref, sketch, basis,
-    sem_in, sem_r, sem_proj, sems, early_sems,
+    steps, early, cells, own_ref, theirs_ref, both_ref, sketch, r_hbm, basis_hbm, proj_hbm,
+    a_ref, one_ref, low_r_ref, low_x_ref, r_ref, x_ref, proj_ref, basis,
+    sem_r, sem_proj, sems, early_sems,
 ):
-    copy_in = pltpu.make_async_copy(sketch_hbm, sketch, sem_in)
-    copy_in.start()
     k = r_ref.shape[0]
     n = k // 2
     one_ref[...] = jnp.ones_like(one_ref)
@@ -363,8 +361,6 @@
     copies = []
 
     def first_columns(panel):
-        if panel == 1:
-            copy_in.wait()
         index = panel - 2
         if not 0 <= index < early:
             return
@@ -442,7 +438,7 @@
             jax.ShapeDtypeStruct((rows, k), jnp.bfloat16),
             jax.ShapeDtypeStruct((days, k // cells), jnp.float32),
         ),
-        in_specs=[vmem, vmem, vmem, hbm],
+        in_specs=[vmem, vmem, vmem, vmem],
         out_specs=(hbm, hbm, hbm),
         scratch_shapes=[
             pltpu.VMEM((n, n), jnp.float32),
@@ -452,9 +448,7 @@
             pltpu.VMEM((k, k), jnp.float32),
             pltpu.VMEM((k, k), jnp.float32),
             pltpu.VMEM((days, k // cells), jnp.float32),
-            pltpu.VMEM((rows, k), sketch.dtype),
             pltpu.VMEM((rows, k), jnp.bfloat16),
-            pltpu.SemaphoreType.DMA,
             pltpu.SemaphoreType.DMA,
             pltpu.SemaphoreType.DMA,
             pltpu.SemaphoreType.DMA((steps,)),

time: 28.1 us -> 27.9 us (level)
  no operation moved by 1% of the time
where the time goes in v7:
time: 27.9 us; the launch traced here: 27.8 us
  waiting for transfers between devices  10.7 us (38%)
  starting transfers between devices  9.05 us (32%)
  Pallas kernels  7.19 us (26%)
  between operations  0.7 us (3%)
    ppermute x5, waiting for transfers between devices, swap(): return lax.ppermute(value, axis, [(i, i ^ bit) for i in range(size)])  10.7 us
    ppermute x5, starting transfers between devices, swap(): return lax.ppermute(value, axis, [(i, i ^ bit) for i in range(size)])  9.05 us
    pallas_call x1, Pallas kernels, factor_rest(): pl.pallas_call(functools.partial(rest_kernel, steps, early, cells), out_s...  4.82 us
    pallas_call x1, Pallas kernels, local_stats(): pl.pallas_call(functools.partial(stats_kernel, steps, groups), out_shape=...  2.35 us
  transfers between devices with their start and end apart: 5, of which 5 were waited for; matrix products, arithmetic and copies ran while one was open for 0% of the time, Pallas kernels for 0%

profile of v7, /device:TPU:0, one launch (start us, length us, event | category | flops | bytes accessed | tf_op | source)
XLA Modules:
  0.0 27.8 jit_solution(10940648233596587361)
XLA Ops:
  0.6 2.3 %local_stats.1 = (f32[264,128]{1,0:T(8,128)S(1)}, f32[264,128]{1,0:T(8,128)S(1)}) custom-call(bf16[3072,256]{1,0:T(8,128)(2,1)} %sketch.1, bf16[3072,128]{1,0:T(8,128)(2,1)} %slab_hbm.1), custom_call_target="tpu_custom_call" | custom-call | tf_op jit(solution)/shard_map/local_stats/pallas_call | solution.py:80
  3.0 0.0 copy-start
  3.0 0.5 %collective-permute-start = (f32[264,128]{1,0:T(8,128)S(1)}, f32[264,128]{1,0:T(8,128)S(1)}, u32[]{:S(2)}, u32[]{:S(2)}) collective-permute-start(f32[264,128]{1,0:T(8,128)S(1)} %get-tuple-element.9), channel_id=1, source_target_pairs={{0,1},{1,0},{2,3},{3,2},{4,5},{5,4},{6,7},{7,6},{8,9},{9,8},{10,11... | collective-permute-start | bytes 405512 | tf_op jit(solution)/shard_map/ppermute | solution.py:464
  3.5 1.0 %collective-permute-done = f32[264,128]{1,0:T(8,128)S(1)} collective-permute-done((f32[264,128]{1,0:T(8,128)S(1)}, f32[264,128]{1,0:T(8,128)S(1)}, u32[]{:S(2)}, u32[]{:S(2)}) %collective-permute-start) | collective-permute-done | bytes 135200 | tf_op jit(solution)/shard_map/ppermute | solution.py:464
  4.6 2.9 %collective-permute-start.1 = (f32[200,128]{1,0:T(8,128)S(1)}, f32[200,128]{1,0:T(8,128)S(1)}, u32[]{:S(2)}, u32[]{:S(2)}) collective-permute-start(f32[200,128]{1,0:T(8,128)S(1)} %pad_maximum_fusion), channel_id=1, source_target_pairs={{0,2},{1,3},{2,0},{3,1},{4,6},{5,7},{6,4},{7,5},{8,10},{9,11},{10,... | collective-permute-start | bytes 307208 | tf_op jit(solution)/shard_map/ppermute | solution.py:464
  7.5 3.2 %collective-permute-done.1 = f32[200,128]{1,0:T(8,128)S(1)} collective-permute-done((f32[200,128]{1,0:T(8,128)S(1)}, f32[200,128]{1,0:T(8,128)S(1)}, u32[]{:S(2)}, u32[]{:S(2)}) %collective-permute-start.1) | collective-permute-done | bytes 102432 | tf_op jit(solution)/shard_map/ppermute | solution.py:464
  10.7 1.9 %collective-permute-start.2 = (f32[200,128]{1,0:T(8,128)S(1)}, f32[200,128]{1,0:T(8,128)S(1)}, u32[]{:S(2)}, u32[]{:S(2)}) collective-permute-start(f32[200,128]{1,0:T(8,128)S(1)} %fusion), channel_id=1, source_target_pairs={{0,4},{4,0},{8,12},{12,8},{1,5},{5,1},{9,13},{13,9},{2,6},{6,2},{1... | collective-permute-start | bytes 307208 | tf_op jit(solution)/shard_map/ppermute | solution.py:464
  12.6 2.8 %collective-permute-done.2 = f32[200,128]{1,0:T(8,128)S(1)} collective-permute-done((f32[200,128]{1,0:T(8,128)S(1)}, f32[200,128]{1,0:T(8,128)S(1)}, u32[]{:S(2)}, u32[]{:S(2)}) %collective-permute-start.2) | collective-permute-done | bytes 102432 | tf_op jit(solution)/shard_map/ppermute | solution.py:464
  15.5 2.9 %collective-permute-start.3 = (f32[200,128]{1,0:T(8,128)S(1)}, f32[200,128]{1,0:T(8,128)S(1)}, u32[]{:S(2)}, u32[]{:S(2)}) collective-permute-start(f32[200,128]{1,0:T(8,128)S(1)} %add.30), channel_id=1, source_target_pairs={{0,8},{4,12},{8,0},{12,4},{1,9},{5,13},{9,1},{13,5},{2,10},{6,14},... | collective-permute-start | bytes 307208 | tf_op jit(solution)/shard_map/ppermute | solution.py:464
  18.4 2.7 %collective-permute-done.3 = f32[200,128]{1,0:T(8,128)S(1)} collective-permute-done((f32[200,128]{1,0:T(8,128)S(1)}, f32[200,128]{1,0:T(8,128)S(1)}, u32[]{:S(2)}, u32[]{:S(2)}) %collective-permute-start.3) | collective-permute-done | bytes 102432 | tf_op jit(solution)/shard_map/ppermute | solution.py:464
  21.1 0.8 %collective-permute-start.4 = (f32[256,128]{1,0:T(8,128)S(1)}, f32[256,128]{1,0:T(8,128)S(1)}, u32[]{:S(2)}, u32[]{:S(2)}) collective-permute-start(f32[256,128]{1,0:T(8,128)S(1)} %factor_top.1.own_ref), channel_id=1, source_target_pairs={{0,1},{1,0},{2,3},{3,2},{4,5},{5,4},{6,7},{7,6},{8,9},{9,8},{10,11... | collective-permute-start | bytes 393224 | tf_op jit(solution)/shard_map/ppermute | solution.py:464
  22.0 1.0 %collective-permute-done.4.theirs_ref = f32[256,128]{1,0:T(8,128)S(1)} collective-permute-done((f32[256,128]{1,0:T(8,128)S(1)}, f32[256,128]{1,0:T(8,128)S(1)}, u32[]{:S(2)}, u32[]{:S(2)}) %collective-permute-start.4) | collective-permute-done | bytes 131104 | tf_op jit(solution)/shard_map/ppermute | solution.py:464
  23.0 0.0 copy-done
  23.0 4.8 %factor_rest.1 = (f32[256,256]{1,0:T(8,128)}, bf16[3072,256]{1,0:T(8,128)(2,1)}, f32[32,64]{1,0:T(8,128)}) custom-call(f32[256,128]{1,0:T(8,128)S(1)} %factor_top.1.own_ref, f32[256,128]{1,0:T(8,128)S(1)} %collective-permute-done.4.theirs_ref, f32[200,128]{1,0:T(8,128)S(1)} %add.31.both_ref, bf16[3072,256]{1,0:T(8,128)(2,1)S(1)} %copy-done), custom_call_target="tpu_custom_call" | custom-call | tf_op jit(solution)/shard_map/factor_rest/pallas_call | solution.py:434
  (9 shorter events, 0.1 us)
Async XLA Ops:
  3.0 20.0 %copy-start = (bf16[3072,256]{1,0:T(8,128)(2,1)S(1)}, bf16[3072,256]{1,0:T(8,128)(2,1)}, u32[]{:S(2)}) copy-start(bf16[3072,256]{1,0:T(8,128)(2,1)} %sketch.1) | copy-start | bytes 4718596
  3.0 1.5 %collective-permute-start = (f32[264,128]{1,0:T(8,128)S(1)}, f32[264,128]{1,0:T(8,128)S(1)}, u32[]{:S(2)}, u32[]{:S(2)}) collective-permute-start(f32[264,128]{1,0:T(8,128)S(1)} %get-tuple-element.9), channel_id=1, source_target_pairs={{0,1},{1,0},{2,3},{3,2},{4,5},{5,4},{6,7},{7,6},{8,9},{9,8},{10,11... | collective-permute-start | bytes 405512 | tf_op jit(solution)/shard_map/ppermute | solution.py:464
  4.6 6.1 %collective-permute-start.1 = (f32[200,128]{1,0:T(8,128)S(1)}, f32[200,128]{1,0:T(8,128)S(1)}, u32[]{:S(2)}, u32[]{:S(2)}) collective-permute-start(f32[200,128]{1,0:T(8,128)S(1)} %pad_maximum_fusion), channel_id=1, source_target_pairs={{0,2},{1,3},{2,0},{3,1},{4,6},{5,7},{6,4},{7,5},{8,10},{9,11},{10,... | collective-permute-start | bytes 307208 | tf_op jit(solution)/shard_map/ppermute | solution.py:464
  10.7 4.7 %collective-permute-start.2 = (f32[200,128]{1,0:T(8,128)S(1)}, f32[200,128]{1,0:T(8,128)S(1)}, u32[]{:S(2)}, u32[]{:S(2)}) collective-permute-start(f32[200,128]{1,0:T(8,128)S(1)} %fusion), channel_id=1, source_target_pairs={{0,4},{4,0},{8,12},{12,8},{1,5},{5,1},{9,13},{13,9},{2,6},{6,2},{1... | collective-permute-start | bytes 307208 | tf_op jit(solution)/shard_map/ppermute | solution.py:464
  15.5 5.6 %collective-permute-start.3 = (f32[200,128]{1,0:T(8,128)S(1)}, f32[200,128]{1,0:T(8,128)S(1)}, u32[]{:S(2)}, u32[]{:S(2)}) collective-permute-start(f32[200,128]{1,0:T(8,128)S(1)} %add.30), channel_id=1, source_target_pairs={{0,8},{4,12},{8,0},{12,4},{1,9},{5,13},{9,1},{13,5},{2,10},{6,14},... | collective-permute-start | bytes 307208 | tf_op jit(solution)/shard_map/ppermute | solution.py:464
  21.1 1.8 %collective-permute-start.4 = (f32[256,128]{1,0:T(8,128)S(1)}, f32[256,128]{1,0:T(8,128)S(1)}, u32[]{:S(2)}, u32[]{:S(2)}) collective-permute-start(f32[256,128]{1,0:T(8,128)S(1)} %factor_top.1.own_ref), channel_id=1, source_target_pairs={{0,1},{1,0},{2,3},{3,2},{4,5},{5,4},{6,7},{7,6},{8,9},{9,8},{10,11... | collective-permute-start | bytes 393224 | tf_op jit(solution)/shard_map/ppermute | solution.py:464

commit v8 on v7

--- a/solution.py
+++ b/solution.py
@@ -403,7 +403,7 @@
         copy = pltpu.make_async_copy(basis.at[rows, at], basis_hbm.at[rows, at], sems.at[step])
         copy.start()
         copies.append(copy)
-        if step:
+        if step != steps // 2:
             continue
         count = k // cells
         own_rows = pl.ds(pl.multiple_of(lax.axis_index("cell") * count, count), count)

time: 27.9 us -> 27.9 us (level)
  no operation moved by 1% of the time
where the time goes in v8:
time: 27.9 us; the launch traced here: 27.8 us
  waiting for transfers between devices  10.7 us (38%)
  starting transfers between devices  9.05 us (32%)
  Pallas kernels  7.17 us (26%)
  between operations  0.7 us (3%)
    ppermute x5, waiting for transfers between devices, swap(): return lax.ppermute(value, axis, [(i, i ^ bit) for i in range(size)])  10.7 us
    ppermute x5, starting transfers between devices, swap(): return lax.ppermute(value, axis, [(i, i ^ bit) for i in range(size)])  9.05 us
    pallas_call x1, Pallas kernels, factor_rest(): pl.pallas_call(functools.partial(rest_kernel, steps, early, cells), out_s...  4.8 us
    pallas_call x1, Pallas kernels, local_stats(): pl.pallas_call(functools.partial(stats_kernel, steps, groups), out_shape=...  2.35 us
  transfers between devices with their start and end apart: 5, of which 5 were waited for; matrix products, arithmetic and copies ran while one was open for 0% of the time, Pallas kernels for 0%

profile of v8, /device:TPU:0, one launch (start us, length us, event | category | flops | bytes accessed | tf_op | source)
XLA Modules:
  0.0 27.8 jit_solution(3561797497187582118)
XLA Ops:
  0.6 2.3 %local_stats.1 = (f32[264,128]{1,0:T(8,128)S(1)}, f32[264,128]{1,0:T(8,128)S(1)}) custom-call(bf16[3072,256]{1,0:T(8,128)(2,1)} %sketch.1, bf16[3072,128]{1,0:T(8,128)(2,1)} %slab_hbm.1), custom_call_target="tpu_custom_call" | custom-call | tf_op jit(solution)/shard_map/local_stats/pallas_call | solution.py:80
  3.0 0.0 copy-start
  3.0 0.5 %collective-permute-start = (f32[264,128]{1,0:T(8,128)S(1)}, f32[264,128]{1,0:T(8,128)S(1)}, u32[]{:S(2)}, u32[]{:S(2)}) collective-permute-start(f32[264,128]{1,0:T(8,128)S(1)} %get-tuple-element.9), channel_id=1, source_target_pairs={{0,1},{1,0},{2,3},{3,2},{4,5},{5,4},{6,7},{7,6},{8,9},{9,8},{10,11... | collective-permute-start | bytes 405512 | tf_op jit(solution)/shard_map/ppermute | solution.py:464
  3.5 1.0 %collective-permute-done = f32[264,128]{1,0:T(8,128)S(1)} collective-permute-done((f32[264,128]{1,0:T(8,128)S(1)}, f32[264,128]{1,0:T(8,128)S(1)}, u32[]{:S(2)}, u32[]{:S(2)}) %collective-permute-start) | collective-permute-done | bytes 135200 | tf_op jit(solution)/shard_map/ppermute | solution.py:464
  4.6 2.9 %collective-permute-start.1 = (f32[200,128]{1,0:T(8,128)S(1)}, f32[200,128]{1,0:T(8,128)S(1)}, u32[]{:S(2)}, u32[]{:S(2)}) collective-permute-start(f32[200,128]{1,0:T(8,128)S(1)} %pad_maximum_fusion), channel_id=1, source_target_pairs={{0,2},{1,3},{2,0},{3,1},{4,6},{5,7},{6,4},{7,5},{8,10},{9,11},{10,... | collective-permute-start | bytes 307208 | tf_op jit(solution)/shard_map/ppermute | solution.py:464
  7.5 3.2 %collective-permute-done.1 = f32[200,128]{1,0:T(8,128)S(1)} collective-permute-done((f32[200,128]{1,0:T(8,128)S(1)}, f32[200,128]{1,0:T(8,128)S(1)}, u32[]{:S(2)}, u32[]{:S(2)}) %collective-permute-start.1) | collective-permute-done | bytes 102432 | tf_op jit(solution)/shard_map/ppermute | solution.py:464
  10.7 1.9 %collective-permute-start.2 = (f32[200,128]{1,0:T(8,128)S(1)}, f32[200,128]{1,0:T(8,128)S(1)}, u32[]{:S(2)}, u32[]{:S(2)}) collective-permute-start(f32[200,128]{1,0:T(8,128)S(1)} %fusion), channel_id=1, source_target_pairs={{0,4},{4,0},{8,12},{12,8},{1,5},{5,1},{9,13},{13,9},{2,6},{6,2},{1... | collective-permute-start | bytes 307208 | tf_op jit(solution)/shard_map/ppermute | solution.py:464
  12.6 2.8 %collective-permute-done.2 = f32[200,128]{1,0:T(8,128)S(1)} collective-permute-done((f32[200,128]{1,0:T(8,128)S(1)}, f32[200,128]{1,0:T(8,128)S(1)}, u32[]{:S(2)}, u32[]{:S(2)}) %collective-permute-start.2) | collective-permute-done | bytes 102432 | tf_op jit(solution)/shard_map/ppermute | solution.py:464
  15.5 2.9 %collective-permute-start.3 = (f32[200,128]{1,0:T(8,128)S(1)}, f32[200,128]{1,0:T(8,128)S(1)}, u32[]{:S(2)}, u32[]{:S(2)}) collective-permute-start(f32[200,128]{1,0:T(8,128)S(1)} %add.30), channel_id=1, source_target_pairs={{0,8},{4,12},{8,0},{12,4},{1,9},{5,13},{9,1},{13,5},{2,10},{6,14},... | collective-permute-start | bytes 307208 | tf_op jit(solution)/shard_map/ppermute | solution.py:464
  18.4 2.7 %collective-permute-done.3 = f32[200,128]{1,0:T(8,128)S(1)} collective-permute-done((f32[200,128]{1,0:T(8,128)S(1)}, f32[200,128]{1,0:T(8,128)S(1)}, u32[]{:S(2)}, u32[]{:S(2)}) %collective-permute-start.3) | collective-permute-done | bytes 102432 | tf_op jit(solution)/shard_map/ppermute | solution.py:464
  21.1 0.8 %collective-permute-start.4 = (f32[256,128]{1,0:T(8,128)S(1)}, f32[256,128]{1,0:T(8,128)S(1)}, u32[]{:S(2)}, u32[]{:S(2)}) collective-permute-start(f32[256,128]{1,0:T(8,128)S(1)} %factor_top.1.own_ref), channel_id=1, source_target_pairs={{0,1},{1,0},{2,3},{3,2},{4,5},{5,4},{6,7},{7,6},{8,9},{9,8},{10,11... | collective-permute-start | bytes 393224 | tf_op jit(solution)/shard_map/ppermute | solution.py:464
  22.0 1.0 %collective-permute-done.4.theirs_ref = f32[256,128]{1,0:T(8,128)S(1)} collective-permute-done((f32[256,128]{1,0:T(8,128)S(1)}, f32[256,128]{1,0:T(8,128)S(1)}, u32[]{:S(2)}, u32[]{:S(2)}) %collective-permute-start.4) | collective-permute-done | bytes 131104 | tf_op jit(solution)/shard_map/ppermute | solution.py:464
  23.0 0.0 copy-done
  23.0 4.8 %factor_rest.1 = (f32[256,256]{1,0:T(8,128)}, bf16[3072,256]{1,0:T(8,128)(2,1)}, f32[32,64]{1,0:T(8,128)}) custom-call(f32[256,128]{1,0:T(8,128)S(1)} %factor_top.1.own_ref, f32[256,128]{1,0:T(8,128)S(1)} %collective-permute-done.4.theirs_ref, f32[200,128]{1,0:T(8,128)S(1)} %add.31.both_ref, bf16[3072,256]{1,0:T(8,128)(2,1)S(1)} %copy-done), custom_call_target="tpu_custom_call" | custom-call | tf_op jit(solution)/shard_map/factor_rest/pallas_call | solution.py:434
  (9 shorter events, 0.1 us)
Async XLA Ops:
  3.0 20.0 %copy-start = (bf16[3072,256]{1,0:T(8,128)(2,1)S(1)}, bf16[3072,256]{1,0:T(8,128)(2,1)}, u32[]{:S(2)}) copy-start(bf16[3072,256]{1,0:T(8,128)(2,1)} %sketch.1) | copy-start | bytes 4718596
  3.0 1.5 %collective-permute-start = (f32[264,128]{1,0:T(8,128)S(1)}, f32[264,128]{1,0:T(8,128)S(1)}, u32[]{:S(2)}, u32[]{:S(2)}) collective-permute-start(f32[264,128]{1,0:T(8,128)S(1)} %get-tuple-element.9), channel_id=1, source_target_pairs={{0,1},{1,0},{2,3},{3,2},{4,5},{5,4},{6,7},{7,6},{8,9},{9,8},{10,11... | collective-permute-start | bytes 405512 | tf_op jit(solution)/shard_map/ppermute | solution.py:464
  4.6 6.1 %collective-permute-start.1 = (f32[200,128]{1,0:T(8,128)S(1)}, f32[200,128]{1,0:T(8,128)S(1)}, u32[]{:S(2)}, u32[]{:S(2)}) collective-permute-start(f32[200,128]{1,0:T(8,128)S(1)} %pad_maximum_fusion), channel_id=1, source_target_pairs={{0,2},{1,3},{2,0},{3,1},{4,6},{5,7},{6,4},{7,5},{8,10},{9,11},{10,... | collective-permute-start | bytes 307208 | tf_op jit(solution)/shard_map/ppermute | solution.py:464
  10.7 4.7 %collective-permute-start.2 = (f32[200,128]{1,0:T(8,128)S(1)}, f32[200,128]{1,0:T(8,128)S(1)}, u32[]{:S(2)}, u32[]{:S(2)}) collective-permute-start(f32[200,128]{1,0:T(8,128)S(1)} %fusion), channel_id=1, source_target_pairs={{0,4},{4,0},{8,12},{12,8},{1,5},{5,1},{9,13},{13,9},{2,6},{6,2},{1... | collective-permute-start | bytes 307208 | tf_op jit(solution)/shard_map/ppermute | solution.py:464
  15.5 5.6 %collective-permute-start.3 = (f32[200,128]{1,0:T(8,128)S(1)}, f32[200,128]{1,0:T(8,128)S(1)}, u32[]{:S(2)}, u32[]{:S(2)}) collective-permute-start(f32[200,128]{1,0:T(8,128)S(1)} %add.30), channel_id=1, source_target_pairs={{0,8},{4,12},{8,0},{12,4},{1,9},{5,13},{9,1},{13,5},{2,10},{6,14},... | collective-permute-start | bytes 307208 | tf_op jit(solution)/shard_map/ppermute | solution.py:464
  21.1 1.8 %collective-permute-start.4 = (f32[256,128]{1,0:T(8,128)S(1)}, f32[256,128]{1,0:T(8,128)S(1)}, u32[]{:S(2)}, u32[]{:S(2)}) collective-permute-start(f32[256,128]{1,0:T(8,128)S(1)} %factor_top.1.own_ref), channel_id=1, source_target_pairs={{0,1},{1,0},{2,3},{3,2},{4,5},{5,4},{6,7},{7,6},{8,9},{9,8},{10,11... | collective-permute-start | bytes 393224 | tf_op jit(solution)/shard_map/ppermute | solution.py:464
